TPU v7x, 256 devices: a whole 4x4x8 slice. The times are simulated.
256 devices in a mesh: ma: 64 (over x, z, core), freq: 4 (over y).
Axes of the slice: x: 4, y: 4, z: 8, core: 2. Of those that a mesh axis runs over, the one named last changes fastest.
Arguments:
- visibility: bfloat16 [2048, 2, 2, 1024], P('ma', None, None, 'freq'), may hold values from -6 to 6
- pair_baseline: int32 [4096, 1], replicated, may hold values from 0 to 1023
- beam_inverse: bfloat16 [256, 2, 2, 1024, 1024], P('ma', None, None, None, 'freq'), may hold values from -0.0625 to 0.0625
- block_rows: int32 [256], P('ma'), may hold values from 1 to 1024, as said below
- legendre: bfloat16 [256, 1024, 1024], P('ma', None, 'freq'), may hold values from -0.0078125 to 0.0078125
- circle_pixels: int32 [1024], P(('freq', 'ma')), may hold values from 4 to 2048, as said below
Outputs:
- sky_map: float32 [2, 1024, 2048], P(None, ('freq', 'ma'))
Inputs may be any that keep to these rules, and one draw needn't show every extreme that they name: `pair_baseline`: every baseline is named by at least one feed pair. `block_rows`: 1024 is reached in every draw. `circle_pixels`: 2048 is reached in every draw.
All inputs are finite; a program needn't handle non-finite values.
Results may differ from a plain program's by a relative error of at most 0.006.
Values may be sent and summed in bfloat16 or wider, within the bound.
No kernel may reach another device: no remote copies, remote signals or barrier semaphores. Data moves between devices by JAX's collectives and lax.ppermute only.
A program may use at most 64 MiB of HBM per device.

v0:
```python
import math

import jax
import jax.numpy as jnp
from jax import lax
from jax.experimental import pallas as pl
from jax.experimental.pallas import tpu as pltpu
from jax.sharding import PartitionSpec as P

PMAX = 2048
INNER = 128
OUTER = PMAX // INNER
COS = (
    1.0, -19.739208221435547, 64.93939208984375, -85.45664978027344,
    60.24201202392578, -26.403913497924805, 7.797765254974365, -1.4502166509628296,
)
SIN = (
    6.2831854820251465, -41.34170150756836, 81.6052474975586, -76.70579528808594,
    42.057708740234375, -15.086281776428223, 3.7804296016693115, -0.6196905970573425,
)
BF16 = jnp.bfloat16
F32 = jnp.float32
SMEM = pl.BlockSpec(memory_space=pltpu.SMEM)
VMEM = pl.BlockSpec(memory_space=pltpu.VMEM)


def split(x):
    high = x.astype(BF16)
    return high, (x - high.astype(F32)).astype(BF16)


def iota(shape, dimension):
    return lax.broadcasted_iota(jnp.int32, shape, dimension)


def polynomial(square, terms):
    total = jnp.full_like(square, terms[-1])
    for term in terms[-2::-1]:
        total = total * square + term
    return total


def cos_sin(phase, period, inverse):
    rest = phase - jnp.round(phase * inverse) * period
    turn = rest * inverse
    square = turn * turn
    return polynomial(square, COS), polynomial(square, SIN) * turn


def dot(a, b, contract):
    return lax.dot_general(a, b, ((contract[:1], contract[1:]), ((), ())), preferred_element_type=F32)


def call(kernel, outs, specs, *args, cost=None, name=None):
    args = [
        pltpu.with_memory_space_constraint(a, pltpu.VMEM) if s is VMEM else a
        for a, s in zip(args, specs)
    ]
    flops, size = cost or (1000000, 100000)
    return pl.pallas_call(
        kernel,
        out_shape=tuple(pltpu.VMEM(s, d) for s, d in outs),
        in_specs=list(specs),
        out_specs=tuple(VMEM for _ in outs),
        cost_estimate=pl.CostEstimate(flops=flops, bytes_accessed=size, transcendentals=0),
        compiler_params=pltpu.CompilerParams(vmem_limit_bytes=30 * 1024 * 1024),
        name=name,
    )(*args)


def phase_kernel(time_dev, nfreq, ntime, place_ref, table_ref):
    rows, width = table_ref.shape[1:]
    row = iota((rows, 1), 0)
    column = iota((1, width), 1)
    mode, part_out, freq_out = row // (2 * nfreq), row // nfreq % 2, row % nfreq
    source = jnp.where(column < width // 2, place_ref[0], place_ref[1])
    inside = column % (width // 2)
    time = source * time_dev + inside // (2 * nfreq)
    part_in, freq_in = inside // nfreq % 2, inside % nfreq
    phase = mode * time + (part_out - part_in) * (ntime // 4)
    turn = ((phase + ntime // 2) % ntime - ntime // 2).astype(F32) * (1.0 / ntime)
    value = polynomial(turn * turn, COS) * (1.0 / math.sqrt(ntime))
    value = jnp.where(freq_out == freq_in, value, 0.0)
    table_ref[0], table_ref[1] = split(value)


def time_kernel(table_ref, own_ref, other_ref, out_ref):
    signal = jnp.concatenate([own_ref[...], other_ref[...]], 0)
    total = dot(table_ref[0], signal, (1, 0)) + dot(table_ref[1], signal, (1, 0))
    out_ref[...] = total.reshape(out_ref.shape).astype(BF16)


def beam_kernel(nfreq, part_ref, weight_ref, beam_ref, total_ref, send_ref):
    sources, rows, width = part_ref.shape
    cores = sources // 2
    sums = part_ref[...].astype(F32).reshape(cores, 2, rows, width).sum(0)
    weighted = jnp.concatenate([sums[0], sums[1]], 1) * weight_ref[...]
    row = iota(weighted.shape, 0)
    turned = jnp.where(
        row // nfreq % 2 == 0,
        -pltpu.roll(weighted, rows - nfreq, 0),
        pltpu.roll(weighted, nfreq, 0),
    )
    total = jnp.zeros(total_ref.shape, F32)
    for m in range(beam_ref.shape[0]):
        for f in range(nfreq):
            live = (row // (2 * nfreq) == m) & (row % nfreq == f)
            for c, value in enumerate((weighted, turned)):
                left = jnp.where(live, value, 0.0).astype(BF16)
                total += dot(left, beam_ref[m, f, c], (1, 1))
    total_ref[...] = total
    send_ref[...] = total.astype(BF16)


def legendre_kernel(
    rows_ref, own_ref, first_ref, second_ref, third_ref, table_ref, out_ref, scratch_ref
):
    total = own_ref[...] + first_ref[...].astype(F32)
    total = total + second_ref[...].astype(F32) + third_ref[...].astype(F32)
    modes = table_ref.shape[0]
    each = total.shape[0] // modes
    row = iota(total.shape, 0)
    column = iota(total.shape, 1)
    latitude = jnp.zeros((total.shape[0], table_ref.shape[2]), F32)
    for m in range(modes):
        live = (row // each == m) & (column < rows_ref[m])
        latitude += dot(jnp.where(live, total, 0.0).astype(BF16), table_ref[m], (1, 0))
    scratch_ref[...] = latitude.astype(BF16).astype(F32).T
    dests, _, width = out_ref.shape
    circles = scratch_ref.shape[0] // dests
    pieces = [scratch_ref[pl.ds(j, dests, circles), :] for j in range(circles)]
    out_ref[...] = jnp.concatenate(pieces, 1).reshape(out_ref.shape)


def mode_of(position, modes, mode_dev):
    blocks = modes // mode_dev
    return position % blocks * mode_dev + position // blocks


def table_kernel(modes, mode_dev, count_ref, outer_ref, inner_ref):
    for circle in range(count_ref.shape[0]):
        period = jnp.full((1, 1), 2 * count_ref[circle], jnp.int32).astype(F32)
        inverse = 1.0 / period
        mode = mode_of(iota((OUTER, modes), 1), modes, mode_dev)
        step = iota((OUTER, modes), 0) * (2 * INNER)
        outer_ref[circle, 0], outer_ref[circle, 1] = cos_sin(
            (mode * step).astype(F32), period, inverse
        )
        mode = mode_of(iota((modes, INNER), 0), modes, mode_dev)
        step = iota((modes, INNER), 1) * 2 + 1
        cosine, sine = cos_sin((mode * step).astype(F32), period, inverse)
        factor = jnp.where(mode == 0, 1.0, 2.0)
        for part, value in enumerate((cosine * factor, -sine * factor)):
            high, low = split(value)
            inner_ref[circle, part * modes : (part + 1) * modes, :INNER] = high
            inner_ref[circle, part * modes : (part + 1) * modes, INNER:] = low


def synthesis_kernel(nfreq, count_ref, value_ref, outer_ref, inner_ref, map_ref):
    circles = outer_ref.shape[0]
    sources, _, width = value_ref.shape
    values = value_ref[...].reshape(sources, width).T
    each = width // circles
    wide = 2 * nfreq
    results = []
    for circle in range(circles):
        block = values[circle * each : (circle + 1) * each]
        block = jnp.concatenate([block[i : i + wide] for i in range(0, each, wide)], 1)
        cosine = outer_ref[circle, 0]
        sine = outer_ref[circle, 1]
        rows = []
        for f in range(nfreq):
            real = block[f : f + 1]
            imag = block[nfreq + f : nfreq + f + 1]
            rows.append(
                jnp.concatenate([real * cosine - imag * sine, real * sine + imag * cosine], 1)
            )
        high, low = split(jnp.concatenate(rows, 0))
        result = dot(jnp.concatenate([high, low], 0), inner_ref[circle], (1, 0))
        half = nfreq * OUTER
        results.append(
            result[:half, :INNER] + (result[:half, INNER:] + result[half:, :INNER])
        )
    pixel = iota((OUTER, INNER), 0) * INNER + iota((OUTER, INNER), 1)
    for circle in range(circles):
        keep = pixel < count_ref[circle]
        for f in range(nfreq):
            part = jnp.where(keep, results[circle][f * OUTER : (f + 1) * OUTER], 0.0)
            for q in range(OUTER):
                map_ref[f, circle : circle + 1, q * INNER : (q + 1) * INNER] = part[q : q + 1]


def body(visibility, pair_baseline, beam_inverse, block_rows, legendre, circle_pixels):
    ma_count = lax.axis_size("ma")
    freq_count = lax.axis_size("freq")
    ma_place = lax.axis_index("ma")
    freq_place = lax.axis_index("freq")
    time_dev, _, nfreq, base_dev = visibility.shape
    ntime = time_dev * ma_count
    mode_dev, _, _, lrows, _ = beam_inverse.shape
    modes = mode_dev * ma_count
    circles = circle_pixels.shape[0]
    base_half = base_dev // 2
    core = ma_place % 2
    rows = mode_dev * 2 * nfreq

    def half(which):
        piece = lax.dynamic_slice_in_dim(visibility, which * base_half, base_half, 3)
        return piece.reshape(time_dev * 2 * nfreq, base_half)

    other = lax.ppermute(half(1 - core), "ma", [(i, i ^ 1) for i in range(ma_count)])
    place = jnp.stack([ma_place, ma_place + 1 - 2 * core]).astype(jnp.int32)
    (table,) = call(
        lambda *refs: phase_kernel(time_dev, nfreq, ntime, *refs),
        [((2, modes * 2 * nfreq, 4 * time_dev * nfreq), BF16)],
        [SMEM],
        place,
        cost=(5000000, 1000000), name="phases",
    )
    (partial_spectrum,) = call(
        time_kernel,
        [((ma_count, rows, base_half), BF16)],
        [VMEM, VMEM, VMEM],
        table, half(core), other, name="time_sum",
    )
    received = lax.all_to_all(partial_spectrum, "ma", 0, 0)

    outer, inner = call(
        lambda *refs: table_kernel(modes, mode_dev, *refs),
        [((circles, 2, OUTER, modes), F32), ((circles, 2 * modes, 2 * INNER), BF16)],
        [SMEM],
        circle_pixels,
        cost=(10000000, 1200000), name="circle_tables",
    )
    base_ids = freq_place * base_dev + jnp.arange(base_dev, dtype=jnp.int32)
    weight = jnp.sqrt(jnp.sum((pair_baseline == base_ids[None, :]).astype(F32), 0))[None, :]

    own, send = call(
        lambda *refs: beam_kernel(nfreq, *refs),
        [((rows, lrows), F32), ((rows, lrows), BF16)],
        [VMEM, VMEM, VMEM],
        received, weight, beam_inverse,
        cost=(300000000, 17000000), name="beam",
    )
    arrived = [
        lax.ppermute(send, "freq", [(i, (i + k) % freq_count) for i in range(freq_count)])
        for k in range(1, freq_count)
    ]
    latitude = pl.pallas_call(
        legendre_kernel,
        out_shape=(pltpu.VMEM((ma_count, 1, circles * rows), F32),),
        in_specs=[SMEM] + [VMEM] * 5,
        out_specs=(VMEM,),
        scratch_shapes=[pltpu.VMEM((legendre.shape[2], rows), F32)],
        name="legendre",
    )(
        block_rows,
        *(
            pltpu.with_memory_space_constraint(a, pltpu.VMEM)
            for a in (own, *arrived, legendre)
        ),
    )[0]
    regrouped = lax.all_to_all(latitude, "ma", 0, 0)
    return pl.pallas_call(
        lambda *refs: synthesis_kernel(nfreq, *refs),
        out_shape=jax.ShapeDtypeStruct((nfreq, circles, PMAX), F32),
        in_specs=[SMEM, VMEM, VMEM, VMEM],
        out_specs=VMEM,
        name="synthesis",
    )(
        circle_pixels,
        *(pltpu.with_memory_space_constraint(a, pltpu.VMEM) for a in (regrouped, outer, inner)),
    )


def solution(mesh):
    return jax.shard_map(
        body,
        mesh=mesh,
        in_specs=(
            P("ma", None, None, "freq"),
            P(),
            P("ma", None, None, None, "freq"),
            P("ma"),
            P("ma", None, "freq"),
            P(("freq", "ma")),
        ),
        out_specs=P(None, ("freq", "ma"), None),
        check_vma=False,
    )
```

profile of v0, /device:TPU:1, one launch (start us, length us, event | category | flops | bytes accessed | tf_op | source)
XLA Modules:
  0.0 62.2 jit_solution(17675681052285080004)
XLA Ops:
  0.0 0.8 %constant_dynamic-slice_fusion = (bf16[32,2,2,128]{3,2,1,0:T(2,128)(2,1)S(1)}, bf16[32,2,2,128]{3,2,1,0:T(2,128)(2,1)S(1)}) fusion(bf16[32,2,2,256]{3,2,1,0:T(2,128)(2,1)} %param.6, s32[]{:T(128)S(6)} %select_n.15, s32[]{:T(128)S(6)} %select_n.14), kind=kLoop, calls=%fused_computation.3 | loop fusion | bytes 131080 | tf_op jit(solution)/shard_map/dynamic_slice | solution.py:208
  0.8 3.3 %collective-permute-start = (bf16[128,128]{1,0:T(8,128)(2,1)S(1)}, bf16[128,128]{1,0:T(8,128)(2,1)S(1)}, u32[]{:S(2)}, u32[]{:S(2)}) collective-permute-start(bf16[128,128]{1,0:T(8,128)(2,1)S(1)} %bitcast.8), channel_id=1, source_target_pairs={{0,4},{4,0},{8,12},{12,8},{16,20},{20,16},{24,28},{28,24},{32,36},... | collective-permute-start | bytes 98312 | tf_op jit(solution)/shard_map/ppermute | solution.py:211
  4.2 0.1 pad_add_fusion.refs_0_
  4.2 2.0 %phases.1.table_ref = bf16[2,1024,256]{2,1,0:T(8,128)(2,1)S(1)} custom-call(s32[2]{0:T(128)S(1)} %pad_add_fusion.refs_0_), custom_call_target="tpu_custom_call" | custom-call | flops 5000000 | bytes 1000000 | tf_op jit(solution)/shard_map/phases/pallas_call | solution.py:60
  6.3 0.0 collective-permute-done.other_ref
  6.3 1.1 %time_sum.1 = bf16[64,16,128]{2,1,0:T(8,128)(2,1)} custom-call(bf16[2,1024,256]{2,1,0:T(8,128)(2,1)S(1)} %phases.1.table_ref, bf16[128,128]{1,0:T(8,128)(2,1)S(1)} %bitcast.6, bf16[128,128]{1,0:T(8,128)(2,1)S(1)} %collective-permute-done.other_ref), custom_call_target="tpu_custom_call" | custom-call | flops 1000000 | bytes 100000 | tf_op jit(solution)/shard_map/time_sum/pallas_call | solution.py:60
  7.4 9.9 %all-to-all-start = ((bf16[64,16,128]{2,1,0:T(8,128)(2,1)}), bf16[64,16,128]{2,1,0:T(8,128)(2,1)S(1)}, u32[]{:S(2)}, u32[]{:S(2)}) async-start(bf16[64,16,128]{2,1,0:T(8,128)(2,1)} %time_sum.1), calls=%async_computation | async-start | bytes 524288 | tf_op jit(solution)/shard_map/all_to_all | solution.py:226
  17.3 2.5 %convert_reduce_fusion = f32[256]{0:T(256)S(1)} fusion(s32[256]{0:T(256)S(1)} %iota_add_fusion, s32[4096]{0:T(1024)} %bitcast.9), kind=kLoop, calls=%fused_computation | loop fusion | flops 3145472 | bytes 18432 | tf_op jit(solution)/shard_map/reduce_sum | solution.py:236
  19.8 9.5 %all-to-all-done.refs_0_ = bf16[64,16,128]{2,1,0:T(8,128)(2,1)S(1)} async-done(((bf16[64,16,128]{2,1,0:T(8,128)(2,1)}), bf16[64,16,128]{2,1,0:T(8,128)(2,1)S(1)}, u32[]{:S(2)}, u32[]{:S(2)}) %all-to-all-start) | async-done | bytes 262176 | tf_op jit(solution)/shard_map/all_to_all | solution.py:226
  29.3 3.4 %copy-done = bf16[4,2,2,1024,256]{4,3,2,1,0:T(8,128)(2,1)S(1)} copy-done((bf16[4,2,2,1024,256]{4,3,2,1,0:T(8,128)(2,1)S(1)}, bf16[4,2,2,1024,256]{4,3,2,1,0:T(8,128)(2,1)}, u32[]{:S(2)}) %copy-start) | copy-done | bytes 8388632
  32.7 2.2 %beam.1 = (f32[16,1024]{1,0:T(8,128)S(1)}, bf16[16,1024]{1,0:T(8,128)(2,1)S(1)}) custom-call(bf16[64,16,128]{2,1,0:T(8,128)(2,1)S(1)} %all-to-all-done.refs_0_, f32[1,256]{1,0:T(1,128)S(1)} %bitcast.7, bf16[4,2,2,1024,256]{4,3,2,1,0:T(8,128)(2,1)S(1)} %copy-done), custom_call_target="tpu_custom_call" | custom-call | flops 300000000 | bytes 17000000 | tf_op jit(solution)/shard_map/beam/pallas_call | solution.py:60
  34.9 1.3 %collective-permute-start.1 = (bf16[16,1024]{1,0:T(8,128)(2,1)S(1)}, bf16[16,1024]{1,0:T(8,128)(2,1)S(1)}, u32[]{:S(2)}, u32[]{:S(2)}) collective-permute-start(bf16[16,1024]{1,0:T(8,128)(2,1)S(1)} %get-tuple-element.10), channel_id=1, source_target_pairs={{0,1},{1,2},{2,3},{3,0},{4,5},{5,6},{6,7},{7,4},{8,9},{9,10},{10,1... | collective-permute-start | bytes 98312 | tf_op jit(solution)/shard_map/ppermute | solution.py:246
  36.2 2.6 %collective-permute-start.2 = (bf16[16,1024]{1,0:T(8,128)(2,1)S(1)}, bf16[16,1024]{1,0:T(8,128)(2,1)S(1)}, u32[]{:S(2)}, u32[]{:S(2)}) collective-permute-start(bf16[16,1024]{1,0:T(8,128)(2,1)S(1)} %get-tuple-element.10), channel_id=1, source_target_pairs={{0,2},{1,3},{2,0},{3,1},{4,6},{5,7},{6,4},{7,5},{8,10},{9,11},{10,... | collective-permute-start | bytes 98312 | tf_op jit(solution)/shard_map/ppermute | solution.py:246
  38.9 1.1 %collective-permute-start.3 = (bf16[16,1024]{1,0:T(8,128)(2,1)S(1)}, bf16[16,1024]{1,0:T(8,128)(2,1)S(1)}, u32[]{:S(2)}, u32[]{:S(2)}) collective-permute-start(bf16[16,1024]{1,0:T(8,128)(2,1)S(1)} %get-tuple-element.10), channel_id=1, source_target_pairs={{0,3},{1,0},{2,1},{3,2},{4,7},{5,4},{6,5},{7,6},{8,11},{9,8},{10,9... | collective-permute-start | bytes 98312 | tf_op jit(solution)/shard_map/ppermute | solution.py:246
  39.9 0.0 collective-permute-done.1.first_ref
  39.9 0.6 collective-permute-done.2.second_ref
  40.5 1.4 %collective-permute-done.3.third_ref = bf16[16,1024]{1,0:T(8,128)(2,1)S(1)} collective-permute-done((bf16[16,1024]{1,0:T(8,128)(2,1)S(1)}, bf16[16,1024]{1,0:T(8,128)(2,1)S(1)}, u32[]{:S(2)}, u32[]{:S(2)}) %collective-permute-start.3) | collective-permute-done | bytes 32800 | tf_op jit(solution)/shard_map/ppermute | solution.py:246
  41.9 0.0 copy-done.1
  41.9 1.9 %legendre.1 = f32[64,1,64]{2,1,0:T(1,128)} custom-call(s32[4]{0:T(128)} %rows_ref.1, f32[16,1024]{1,0:T(8,128)S(1)} %get-tuple-element.9.own_ref, bf16[16,1024]{1,0:T(8,128)(2,1)S(1)} %collective-permute-done.1.first_ref, bf16[16,1024]{1,0:T(8,128)(2,1)S(1)} %collective-permute-done.2.second_ref, bf16[16,1024]{1,0:T(8,128)(2,1)S(1)} %collective-permute-done.3.third_ref, ...), custom_call_target="tpu_custom_call" | custom-call | tf_op jit(solution)/shard_map/legendre/pallas_call | solution.py:249
  43.8 7.4 %all-to-all-start.1 = ((f32[64,1,64]{2,1,0:T(1,128)}), f32[64,1,64]{2,1,0:T(1,128)S(1)}, u32[]{:S(2)}, u32[]{:S(2)}) async-start(f32[64,1,64]{2,1,0:T(1,128)} %legendre.1), calls=%async_computation.1 | async-start | bytes 65536 | tf_op jit(solution)/shard_map/all_to_all | solution.py:263
  51.3 0.0 copy-done.2
  51.3 1.5 %circle_tables.1 = (f32[4,2,16,256]{3,2,1,0:T(8,128)S(1)}, bf16[4,512,256]{2,1,0:T(8,128)(2,1)S(1)}) custom-call(s32[4]{0:T(128)S(1)} %copy-done.2), custom_call_target="tpu_custom_call" | custom-call | flops 10000000 | bytes 1200000 | tf_op jit(solution)/shard_map/circle_tables/pallas_call | solution.py:60
  52.8 7.7 %all-to-all-done.1.refs_1_ = f32[64,1,64]{2,1,0:T(1,128)S(1)} async-done(((f32[64,1,64]{2,1,0:T(1,128)}), f32[64,1,64]{2,1,0:T(1,128)S(1)}, u32[]{:S(2)}, u32[]{:S(2)}) %all-to-all-start.1) | async-done | bytes 16416 | tf_op jit(solution)/shard_map/all_to_all | solution.py:263
  60.5 1.7 %synthesis.1 = f32[2,4,2048]{2,1,0:T(4,128)} custom-call(s32[4]{0:T(128)} %refs_0_.3, f32[64,1,64]{2,1,0:T(1,128)S(1)} %all-to-all-done.1.refs_1_, f32[4,2,16,256]{3,2,1,0:T(8,128)S(1)} %get-tuple-element.11.refs_2_, bf16[4,512,256]{2,1,0:T(8,128)(2,1)S(1)} %get-tuple-element.12.refs_3_), custom_call_target="tpu_custom_call" | custom-call | tf_op jit(solution)/shard_map/synthesis/pallas_call | solution.py:264
  (5 shorter events, 0.0 us)
Async XLA Ops:
  0.8 5.4 %collective-permute-start = (bf16[128,128]{1,0:T(8,128)(2,1)S(1)}, bf16[128,128]{1,0:T(8,128)(2,1)S(1)}, u32[]{:S(2)}, u32[]{:S(2)}) collective-permute-start(bf16[128,128]{1,0:T(8,128)(2,1)S(1)} %bitcast.8), channel_id=1, source_target_pairs={{0,4},{4,0},{8,12},{12,8},{16,20},{20,16},{24,28},{28,24},{32,36},... | collective-permute-start | bytes 98312 | tf_op jit(solution)/shard_map/ppermute | solution.py:211
  7.4 21.9 %all-to-all-start = ((bf16[64,16,128]{2,1,0:T(8,128)(2,1)}), bf16[64,16,128]{2,1,0:T(8,128)(2,1)S(1)}, u32[]{:S(2)}, u32[]{:S(2)}) async-start(bf16[64,16,128]{2,1,0:T(8,128)(2,1)} %time_sum.1), calls=%async_computation | async-start | bytes 524288 | tf_op jit(solution)/shard_map/all_to_all | solution.py:226
  29.3 3.4 %copy-start = (bf16[4,2,2,1024,256]{4,3,2,1,0:T(8,128)(2,1)S(1)}, bf16[4,2,2,1024,256]{4,3,2,1,0:T(8,128)(2,1)}, u32[]{:S(2)}) copy-start(bf16[4,2,2,1024,256]{4,3,2,1,0:T(8,128)(2,1)} %refs_2_.1) | copy-start | bytes 25165828
  32.7 9.3 %copy-start.1 = (bf16[4,1024,256]{2,1,0:T(8,128)(2,1)S(1)}, bf16[4,1024,256]{2,1,0:T(8,128)(2,1)}, u32[]{:S(2)}) copy-start(bf16[4,1024,256]{2,1,0:T(8,128)(2,1)} %table_ref.1) | copy-start | bytes 6291460
  32.7 18.6 %copy-start.2 = (s32[4]{0:T(128)S(1)}, s32[4]{0:T(128)}, u32[]{:S(2)}) copy-start(s32[4]{0:T(128)} %refs_0_.3) | copy-start | bytes 52
  34.9 5.0 %collective-permute-start.1 = (bf16[16,1024]{1,0:T(8,128)(2,1)S(1)}, bf16[16,1024]{1,0:T(8,128)(2,1)S(1)}, u32[]{:S(2)}, u32[]{:S(2)}) collective-permute-start(bf16[16,1024]{1,0:T(8,128)(2,1)S(1)} %get-tuple-element.10), channel_id=1, source_target_pairs={{0,1},{1,2},{2,3},{3,0},{4,5},{5,6},{6,7},{7,4},{8,9},{9,10},{10,1... | collective-permute-start | bytes 98312 | tf_op jit(solution)/shard_map/ppermute | solution.py:246
  36.2 4.3 %collective-permute-start.2 = (bf16[16,1024]{1,0:T(8,128)(2,1)S(1)}, bf16[16,1024]{1,0:T(8,128)(2,1)S(1)}, u32[]{:S(2)}, u32[]{:S(2)}) collective-permute-start(bf16[16,1024]{1,0:T(8,128)(2,1)S(1)} %get-tuple-element.10), channel_id=1, source_target_pairs={{0,2},{1,3},{2,0},{3,1},{4,6},{5,7},{6,4},{7,5},{8,10},{9,11},{10,... | collective-permute-start | bytes 98312 | tf_op jit(solution)/shard_map/ppermute | solution.py:246
  38.9 3.1 %collective-permute-start.3 = (bf16[16,1024]{1,0:T(8,128)(2,1)S(1)}, bf16[16,1024]{1,0:T(8,128)(2,1)S(1)}, u32[]{:S(2)}, u32[]{:S(2)}) collective-permute-start(bf16[16,1024]{1,0:T(8,128)(2,1)S(1)} %get-tuple-element.10), channel_id=1, source_target_pairs={{0,3},{1,0},{2,1},{3,2},{4,7},{5,4},{6,5},{7,6},{8,11},{9,8},{10,9... | collective-permute-start | bytes 98312 | tf_op jit(solution)/shard_map/ppermute | solution.py:246
  43.8 16.7 %all-to-all-start.1 = ((f32[64,1,64]{2,1,0:T(1,128)}), f32[64,1,64]{2,1,0:T(1,128)S(1)}, u32[]{:S(2)}, u32[]{:S(2)}) async-start(f32[64,1,64]{2,1,0:T(1,128)} %legendre.1), calls=%async_computation.1 | async-start | bytes 65536 | tf_op jit(solution)/shard_map/all_to_all | solution.py:263
where the time goes:
time: 62.6 us; the launch traced here: 62.2 us
  starting transfers between devices  25.6 us (41%)
  waiting for transfers between devices  19.2 us (31%)
  Pallas kernels  10.5 us (17%)
  local copies, waits for them, and re-layouts  4.22 us (7%)
  other arithmetic  2.56 us (4%)
    all_to_all x1, starting transfers between devices, body(): received = lax.all_to_all(partial_spectrum, 'ma', 0, 0)  9.86 us
    all_to_all x1, waiting for transfers between devices, body(): received = lax.all_to_all(partial_spectrum, 'ma', 0, 0)  9.49 us
    all_to_all x1, waiting for transfers between devices, body(): regrouped = lax.all_to_all(latitude, 'ma', 0, 0)  7.71 us
    all_to_all x1, starting transfers between devices, body(): regrouped = lax.all_to_all(latitude, 'ma', 0, 0)  7.44 us
    pallas_call x4, Pallas kernels, call(): pl.pallas_call(kernel, out_shape=tuple((pltpu.VMEM(s, d) for s, d in outs...  6.9 us
    ppermute x3, starting transfers between devices, body(): lax.ppermute(send, 'freq', [(i, (i + k) % freq_count) for i in range(freq...  5.01 us
    unnamed x6, local copies, waits for them, and re-layouts  3.39 us
    ppermute x1, starting transfers between devices, body(): lax.ppermute(half(1 - core), 'ma', [(i, i ^ 1) for i in range(ma_count)])  3.33 us
  transfers between devices with their start and end apart: 6, of which 4 were waited for; matrix products, arithmetic and copies ran while one was open for 4% of the time, Pallas kernels for 6%

commit v1 on v0

v1 whole, which is shorter than its diff:
```python
import math

import jax
import jax.numpy as jnp
import ml_dtypes
import numpy as np
from jax import lax
from jax.experimental import pallas as pl
from jax.experimental.pallas import tpu as pltpu
from jax.sharding import PartitionSpec as P

PMAX = 2048
INNER = 128
OUTER = PMAX // INNER
NEAR = 3
COS = (
    1.0, -19.739208221435547, 64.93939208984375, -85.45664978027344,
    60.24201202392578, -26.403913497924805, 7.797765254974365, -1.4502166509628296,
)
SIN = (
    6.2831854820251465, -41.34170150756836, 81.6052474975586, -76.70579528808594,
    42.057708740234375, -15.086281776428223, 3.7804296016693115, -0.6196905970573425,
)
BF16 = jnp.bfloat16
F32 = jnp.float32
SMEM = pl.BlockSpec(memory_space=pltpu.SMEM)
VMEM = pl.BlockSpec(memory_space=pltpu.VMEM)
ANY = pl.BlockSpec(memory_space=pl.ANY)
PARAMS = pltpu.CompilerParams(vmem_limit_bytes=16 * 1024 * 1024)


def split(x):
    high = x.astype(BF16)
    return high, (x - high.astype(F32)).astype(BF16)


def iota(shape, dimension):
    return lax.broadcasted_iota(jnp.int32, shape, dimension)


def polynomial(square, terms):
    total = jnp.full_like(square, terms[-1])
    for term in terms[-2::-1]:
        total = total * square + term
    return total


def cos_sin(phase, period, inverse):
    rest = phase - jnp.round(phase * inverse) * period
    turn = rest * inverse
    square = turn * turn
    return polynomial(square, COS), polynomial(square, SIN) * turn


def dot(a, b, contract):
    return lax.dot_general(a, b, ((contract[:1], contract[1:]), ((), ())), preferred_element_type=F32)


def call(kernel, outs, specs, *args, name=None):
    args = [
        pltpu.with_memory_space_constraint(a, pltpu.VMEM) if s is VMEM else a
        for a, s in zip(args, specs)
    ]
    return pl.pallas_call(
        kernel,
        out_shape=tuple(pltpu.VMEM(s, d) for s, d in outs),
        in_specs=list(specs),
        out_specs=tuple(VMEM for _ in outs),
        compiler_params=PARAMS,
        name=name,
    )(*args)


def phase_table(modes, nfreq, chip_times, ntime):
    row = np.arange(2 * modes * nfreq)[:, None]
    column = np.arange(chip_times * 2 * nfreq)[None, :]
    part_out, mode, freq_out = row // (modes * nfreq), row // nfreq % modes, row % nfreq
    time, part_in, freq_in = column // (2 * nfreq), column // nfreq % 2, column % nfreq
    phase = (mode * time + (part_out - part_in) * (ntime // 4)) % ntime
    value = np.cos(phase * (2.0 * math.pi / ntime)) / math.sqrt(ntime) * (freq_out == freq_in)
    high = value.astype(ml_dtypes.bfloat16)
    low = (value - high.astype(np.float64)).astype(ml_dtypes.bfloat16)
    return np.stack([high, low])


def fetch_kernel(place_ref, table_ref, signal_ref, near_ref, own_ref, semaphores):
    width = own_ref.shape[3]
    start = pl.multiple_of(place_ref[0] % 2 * width, width)
    copies = [
        pltpu.make_async_copy(
            signal_ref.at[:, :, :, pl.ds(start, width)], own_ref, semaphores.at[0]
        ),
        pltpu.make_async_copy(table_ref, near_ref, semaphores.at[1]),
    ]
    for copy in copies:
        copy.start()
    for copy in copies:
        copy.wait()


def time_kernel(nfreq, chips, place_ref, table_ref, own_ref, other_ref, out_ref):
    even = place_ref[0] % 2 == 0
    own, other = own_ref[...], other_ref[...]
    signal = jnp.concatenate([jnp.where(even, own, other), jnp.where(even, other, own)], 0)
    total = dot(table_ref[0], signal, (1, 0)) + dot(table_ref[1], signal, (1, 0))
    sources, rows, width = out_ref.shape
    phase = iota((chips * nfreq, width), 0) // nfreq * (place_ref[0] // 2)
    turn = ((phase + chips // 2) % chips - chips // 2).astype(F32) * (1.0 / chips)
    square = turn * turn
    cosine, sine = polynomial(square, COS)[None], (polynomial(square, SIN) * turn)[None]
    real, imag = total.reshape(2, -1, chips * nfreq, width)
    shape = (sources, rows // 2, width)
    real, imag = real * cosine + imag * sine, imag * cosine - real * sine
    out_ref[...] = jnp.concatenate([real.reshape(shape), imag.reshape(shape)], 1).astype(BF16)


def side_kernel(nfreq, first_ref, pair_ref, beam_ref, weight_ref, *refs):
    *block_refs, semaphores = refs
    copies = fetch_blocks(nfreq, beam_ref, 0, block_refs, semaphores)
    shape = (weight_ref.shape[1], pair_ref.shape[1])
    ids = iota(shape, 0) + first_ref[0]
    total = jnp.zeros(shape, F32)
    for i in range(pair_ref.shape[0]):
        total += jnp.where(pair_ref[i : i + 1, :] == ids, 1.0, 0.0)
    weight_ref[...] = jnp.sqrt(jnp.sum(total.T, 0, keepdims=True))
    for copy in copies:
        copy.wait()


def fetch_blocks(nfreq, beam_ref, first, block_refs, semaphores):
    copies = [
        pltpu.make_async_copy(
            beam_ref.at[(first + i) // nfreq, (first + i) % nfreq], block_ref, semaphores.at[i]
        )
        for i, block_ref in enumerate(block_refs)
    ]
    for copy in copies:
        copy.start()
    return copies


def beam_kernel(nfreq, part_ref, weight_ref, beam_ref, *refs):
    *near_refs, total_ref, send_ref, far_ref, semaphores = refs
    near = len(near_refs)
    far_refs = [far_ref.at[i] for i in range(far_ref.shape[0])]
    copies = fetch_blocks(nfreq, beam_ref, near, far_refs, semaphores)
    sources, rows, width = part_ref.shape
    half = rows // 2
    sums = part_ref[...].astype(F32).reshape(sources // 2, 2, rows, width).sum(0)
    weighted = jnp.concatenate([sums[0], sums[1]], 1) * weight_ref[...]
    turned = jnp.concatenate([-weighted[half:], weighted[:half]], 0)
    row = iota((2 * rows, weighted.shape[1]), 0) % half
    lefts = [jnp.concatenate(split(value), 0) for value in (weighted, turned)]
    total = jnp.zeros((2 * rows, total_ref.shape[1]), F32)
    for i, block_ref in enumerate([*near_refs, *far_refs]):
        if i >= near:
            copies[i - near].wait()
        for c in range(2):
            left = jnp.where(row == i, lefts[c], jnp.zeros_like(lefts[c]))
            total += dot(left, block_ref[c], (1, 1))
    total = total[:rows] + total[rows:]
    total_ref[...] = total
    send_ref[...] = total.astype(BF16)


def legendre_fetch_kernel(after_ref, table_ref, near_ref, semaphore):
    del after_ref
    copy = pltpu.make_async_copy(table_ref, near_ref, semaphore)
    copy.start()
    copy.wait()


def legendre_kernel(
    nfreq, rows_ref, own_ref, first_ref, second_ref, third_ref, table_ref, out_ref, scratch_ref
):
    total = own_ref[...] + first_ref[...].astype(F32)
    total = total + second_ref[...].astype(F32) + third_ref[...].astype(F32)
    rows = total.shape[0]
    left = jnp.concatenate(split(total), 0)
    row = iota(left.shape, 0) // nfreq
    column = iota(left.shape, 1)
    modes = table_ref.shape[0]
    latitude = jnp.zeros((2 * rows, table_ref.shape[2]), F32)
    for m in range(modes):
        live = (row % modes == m) & (column < rows_ref[m])
        latitude += dot(jnp.where(live, left, jnp.zeros_like(left)), table_ref[m], (1, 0))
    scratch_ref[...] = (latitude[:rows] + latitude[rows:]).T
    dests, _, width = out_ref.shape
    circles = scratch_ref.shape[0] // dests
    pieces = [scratch_ref[pl.ds(j, dests, circles), :] for j in range(circles)]
    out_ref[...] = jnp.concatenate(pieces, 1).reshape(out_ref.shape)


def mode_of(position, modes, mode_dev):
    blocks = modes // mode_dev
    return position % blocks * mode_dev + position // blocks


def table_kernel(modes, mode_dev, count_ref, outer_ref, inner_ref):
    for circle in range(count_ref.shape[0]):
        period = jnp.full((1, 1), 2 * count_ref[circle], jnp.int32).astype(F32)
        inverse = 1.0 / period
        mode = mode_of(iota((OUTER, modes), 1), modes, mode_dev)
        step = iota((OUTER, modes), 0) * (2 * INNER)
        outer_ref[circle, 0], outer_ref[circle, 1] = cos_sin(
            (mode * step).astype(F32), period, inverse
        )
        mode = mode_of(iota((modes, INNER), 0), modes, mode_dev)
        step = iota((modes, INNER), 1) * 2 + 1
        cosine, sine = cos_sin((mode * step).astype(F32), period, inverse)
        factor = jnp.where(mode == 0, 1.0, 2.0)
        for part, value in enumerate((cosine * factor, -sine * factor)):
            high, low = split(value)
            inner_ref[circle, part * modes : (part + 1) * modes, :INNER] = high
            inner_ref[circle, part * modes : (part + 1) * modes, INNER:] = low


def synthesis_kernel(nfreq, count_ref, value_ref, outer_ref, inner_ref, map_ref):
    circles = outer_ref.shape[0]
    sources, _, width = value_ref.shape
    values = value_ref[...].reshape(sources, width).T
    each = width // circles
    results = []
    for circle in range(circles):
        cosine = outer_ref[circle, 0]
        sine = outer_ref[circle, 1]
        rows = []
        for f in range(nfreq):
            start = circle * each + f
            real, imag = (
                jnp.concatenate([values[i : i + 1] for i in range(at, at + each // 2, nfreq)], 1)
                for at in (start, start + each // 2)
            )
            rows.append(
                jnp.concatenate([real * cosine - imag * sine, real * sine + imag * cosine], 1)
            )
        high, low = split(jnp.concatenate(rows, 0))
        result = dot(jnp.concatenate([high, low], 0), inner_ref[circle], (1, 0))
        half = nfreq * OUTER
        results.append(
            result[:half, :INNER] + (result[:half, INNER:] + result[half:, :INNER])
        )
    pixel = iota((OUTER, INNER), 0) * INNER + iota((OUTER, INNER), 1)
    for circle in range(circles):
        keep = pixel < count_ref[circle]
        for f in range(nfreq):
            part = jnp.where(keep, results[circle][f * OUTER : (f + 1) * OUTER], 0.0)
            for q in range(OUTER):
                map_ref[f, circle : circle + 1, q * INNER : (q + 1) * INNER] = part[q : q + 1]


def body(visibility, pair_baseline, beam_inverse, block_rows, legendre, circle_pixels):
    ma_count = lax.axis_size("ma")
    freq_count = lax.axis_size("freq")
    ma_place = lax.axis_index("ma")
    freq_place = lax.axis_index("freq")
    time_dev, _, nfreq, base_dev = visibility.shape
    ntime = time_dev * ma_count
    mode_dev, _, _, lrows, _ = beam_inverse.shape
    modes = mode_dev * ma_count
    circles = circle_pixels.shape[0]
    base_half = base_dev // 2
    rows = mode_dev * 2 * nfreq

    other = lax.ppermute(visibility, "ma", [(i, i ^ 1) for i in range(ma_count)])
    other = lax.dynamic_slice_in_dim(other, ma_place % 2 * base_half, base_half, 3)
    table = jnp.asarray(phase_table(modes, nfreq, 2 * time_dev, ntime))
    near, own = pl.pallas_call(
        fetch_kernel,
        out_shape=(pltpu.VMEM(table.shape, BF16), pltpu.VMEM(other.shape, BF16)),
        in_specs=[SMEM, ANY, ANY],
        out_specs=(VMEM, VMEM),
        scratch_shapes=[pltpu.SemaphoreType.DMA((2,))],
        compiler_params=PARAMS,
        cost_estimate=pl.CostEstimate(flops=0, bytes_accessed=2200000, transcendentals=0),
        name="fetch",
    )(
        ma_place.reshape(1),
        pltpu.with_memory_space_constraint(table, pltpu.HBM),
        pltpu.with_memory_space_constraint(visibility, pltpu.HBM),
    )
    (partial_spectrum,) = call(
        lambda *refs: time_kernel(nfreq, ma_count // 2, *refs),
        [((ma_count, rows, base_half), BF16)],
        [SMEM, VMEM, VMEM, VMEM],
        ma_place.reshape(1),
        near,
        own.reshape(-1, base_half),
        other.reshape(-1, base_half),
        name="time_sum",
    )
    received = lax.all_to_all(partial_spectrum, "ma", 0, 0)

    blocks = mode_dev * nfreq
    block = beam_inverse.shape[2:]
    far_beam = pltpu.with_memory_space_constraint(beam_inverse, pltpu.HBM)
    weight, *near_blocks = pl.pallas_call(
        lambda *refs: side_kernel(nfreq, *refs),
        out_shape=(pltpu.VMEM((1, base_dev), F32),) + (pltpu.VMEM(block, BF16),) * NEAR,
        in_specs=[SMEM, VMEM, ANY],
        out_specs=(VMEM,) * (1 + NEAR),
        scratch_shapes=[pltpu.SemaphoreType.DMA((NEAR,))],
        compiler_params=PARAMS,
        cost_estimate=pl.CostEstimate(
            flops=10000000, bytes_accessed=8 * 1024 * 1024, transcendentals=0
        ),
        name="side",
    )(
        (freq_place * base_dev).reshape(1),
        pltpu.with_memory_space_constraint(pair_baseline.reshape(-1, 128), pltpu.VMEM),
        far_beam,
    )
    own, send = pl.pallas_call(
        lambda *refs: beam_kernel(nfreq, *refs),
        out_shape=(pltpu.VMEM((rows, lrows), F32), pltpu.VMEM((rows, lrows), BF16)),
        in_specs=[VMEM, VMEM, ANY] + [VMEM] * NEAR,
        out_specs=(VMEM, VMEM),
        scratch_shapes=[
            pltpu.VMEM((blocks - NEAR, *block), BF16),
            pltpu.SemaphoreType.DMA((blocks - NEAR,)),
        ],
        compiler_params=PARAMS,
        name="beam",
    )(
        *(pltpu.with_memory_space_constraint(a, pltpu.VMEM) for a in (received, weight)),
        far_beam,
        *(pltpu.with_memory_space_constraint(a, pltpu.VMEM) for a in near_blocks),
    )
    outer, inner = pl.pallas_call(
        lambda *refs: table_kernel(modes, mode_dev, *refs),
        out_shape=(
            pltpu.VMEM((circles, 2, OUTER, modes), F32),
            pltpu.VMEM((circles, 2 * modes, 2 * INNER), BF16),
        ),
        in_specs=[SMEM],
        out_specs=(VMEM, VMEM),
        compiler_params=PARAMS,
        cost_estimate=pl.CostEstimate(flops=10000000, bytes_accessed=1200000, transcendentals=0),
        name="circle_tables",
    )(circle_pixels)
    arrived = [
        lax.ppermute(send, "freq", [(i, (i + k) % freq_count) for i in range(freq_count)])
        for k in range(1, freq_count)
    ]
    near_legendre = pl.pallas_call(
        legendre_fetch_kernel,
        out_shape=(pltpu.VMEM(legendre.shape, BF16),),
        in_specs=[ANY, ANY],
        out_specs=(VMEM,),
        scratch_shapes=[pltpu.SemaphoreType.DMA(())],
        compiler_params=PARAMS,
        cost_estimate=pl.CostEstimate(flops=0, bytes_accessed=4200000, transcendentals=0),
        name="legendre_fetch",
    )(own, pltpu.with_memory_space_constraint(legendre, pltpu.HBM))[0]
    latitude = pl.pallas_call(
        lambda *refs: legendre_kernel(nfreq, *refs),
        out_shape=(pltpu.VMEM((ma_count, 1, circles * rows), F32),),
        in_specs=[SMEM] + [VMEM] * 5,
        out_specs=(VMEM,),
        scratch_shapes=[pltpu.VMEM((legendre.shape[2], rows), F32)],
        compiler_params=PARAMS,
        name="legendre",
    )(
        block_rows,
        *(
            pltpu.with_memory_space_constraint(a, pltpu.VMEM)
            for a in (own, *arrived, near_legendre)
        ),
    )[0]
    regrouped = lax.all_to_all(latitude, "ma", 0, 0)
    return pl.pallas_call(
        lambda *refs: synthesis_kernel(nfreq, *refs),
        out_shape=jax.ShapeDtypeStruct((nfreq, circles, PMAX), F32),
        in_specs=[SMEM, VMEM, VMEM, VMEM],
        out_specs=VMEM,
        compiler_params=PARAMS,
        name="synthesis",
    )(
        circle_pixels,
        *(pltpu.with_memory_space_constraint(a, pltpu.VMEM) for a in (regrouped, outer, inner)),
    )


def solution(mesh):
    return jax.shard_map(
        body,
        mesh=mesh,
        in_specs=(
            P("ma", None, None, "freq"),
            P(),
            P("ma", None, None, None, "freq"),
            P("ma"),
            P("ma", None, "freq"),
            P(("freq", "ma")),
        ),
        out_specs=P(None, ("freq", "ma"), None),
        check_vma=False,
    )
```

time: 62.6 us -> 58 us (0.927)
  local copies, waits for them, and re-layouts: 4.22 us -> 0.05 us
  Pallas kernels: 10.5 us -> 13.8 us
  other arithmetic: 2.56 us -> 0 us
  waiting for transfers between devices: 19.2 us -> 18.1 us
    pallas_call x1 -> x6, Pallas kernels: 1.88 us -> 11 us  [the longest x1 3.01 us: body(): pl.pallas_call(lambda *refs: beam_kernel(nfreq, *refs), out_shape=(pltpu....]
    pallas_call x4 -> x1, Pallas kernels: 6.9 us -> 1.15 us  [call(): pl.pallas_call(kernel, out_shape=tuple((pltpu.VMEM(s, d) for s, d in outs...]
    unnamed x6, local copies, waits for them, and re-layouts: 3.39 us -> 0.01 us
    reduce_sum x1 -> x0, other arithmetic: 2.48 us -> none  [body(): jnp.sum((pair_baseline == base_ids[None, :]).astype(F32), 0)]
    ppermute x3, waiting for transfers between devices: 1.99 us -> 0.34 us  [body(): lax.ppermute(send, 'freq', [(i, (i + k) % freq_count) for i in range(freq...]
    dynamic_slice x1, local copies, waits for them, and re-layouts: 0.82 us -> 0.03 us  [body(): lax.dynamic_slice_in_dim(other, ma_place % 2 * base_half, base_half, 3)]
  transfers between devices with their start and end apart: 6 -> 6, of which waited for: 4 -> 3; matrix products, arithmetic and copies ran while one was open for 4% -> 0% of each run, Pallas kernels for 6% -> 11%
where the time goes in v1:
time: 58 us; the launch traced here: 57.8 us
  starting transfers between devices  25.7 us (44%)
  waiting for transfers between devices  18.1 us (31%)
  Pallas kernels  13.8 us (24%)
    all_to_all x1, waiting for transfers between devices, body(): received = lax.all_to_all(partial_spectrum, 'ma', 0, 0)  10.1 us
    all_to_all x1, starting transfers between devices, body(): received = lax.all_to_all(partial_spectrum, 'ma', 0, 0)  9.92 us
    all_to_all x1, waiting for transfers between devices, body(): regrouped = lax.all_to_all(latitude, 'ma', 0, 0)  7.71 us
    all_to_all x1, starting transfers between devices, body(): regrouped = lax.all_to_all(latitude, 'ma', 0, 0)  7.44 us
    ppermute x3, starting transfers between devices, body(): lax.ppermute(send, 'freq', [(i, (i + k) % freq_count) for i in range(freq...  5.06 us
    ppermute x1, starting transfers between devices, body(): lax.ppermute(visibility, 'ma', [(i, i ^ 1) for i in range(ma_count)])  3.24 us
    pallas_call x1, Pallas kernels, body(): pl.pallas_call(lambda *refs: beam_kernel(nfreq, *refs), out_shape=(pltpu....  3.01 us
    pallas_call x1, Pallas kernels, body(): pl.pallas_call(lambda *refs: side_kernel(nfreq, *refs), out_shape=(pltpu....  1.89 us
  transfers between devices with their start and end apart: 6, of which 3 were waited for; matrix products, arithmetic and copies ran while one was open for 0% of the time, Pallas kernels for 11%

profile of v1, /device:TPU:1, one launch (start us, length us, event | category | flops | bytes accessed | tf_op | source)
XLA Modules:
  0.0 57.8 jit_solution(11403446096581571939)
XLA Ops:
  0.0 3.2 %collective-permute-start = (bf16[32,2,2,256]{3,2,1,0:T(2,128)(2,1)}, bf16[32,2,2,256]{3,2,1,0:T(2,128)(2,1)S(1)}, u32[]{:S(2)}, u32[]{:S(2)}) collective-permute-start(bf16[32,2,2,256]{3,2,1,0:T(2,128)(2,1)} %signal_ref.1), channel_id=1, source_target_pairs={{0,4},{4,0},{8,12},{12,8},{16,20},{20,16},{24,28},{28,24},{32,36},... | collective-permute-start | bytes 196616 | tf_op jit(solution)/shard_map/ppermute | solution.py:265
  3.2 1.3 %fetch.1 = (bf16[2,1024,256]{2,1,0:T(8,128)(2,1)S(1)}, bf16[32,2,2,128]{3,2,1,0:T(2,128)(2,1)S(1)}) custom-call(s32[1]{0:T(128)} %bitcast.place_ref.refs_0_, bf16[2,1024,256]{2,1,0:T(8,128)(2,1)} %constant.29.clone.table_ref, bf16[32,2,2,256]{3,2,1,0:T(2,128)(2,1)} %signal_ref.1), custom_call_target="tpu_custom_call" | custom-call | bytes 2200000 | tf_op jit(solution)/shard_map/fetch/pallas_call | solution.py:268
  4.5 0.0 collective-permute-done
  4.6 1.2 %time_sum.1 = bf16[64,16,128]{2,1,0:T(8,128)(2,1)} custom-call(s32[1]{0:T(128)} %bitcast.place_ref.refs_0_, bf16[2,1024,256]{2,1,0:T(8,128)(2,1)S(1)} %get-tuple-element.15.refs_1_, bf16[128,128]{1,0:T(8,128)(2,1)S(1)} %bitcast.6, bf16[128,128]{1,0:T(8,128)(2,1)S(1)} %bitcast.5), custom_call_target="tpu_custom_call" | custom-call | tf_op jit(solution)/shard_map/time_sum/pallas_call | solution.py:64
  5.7 9.9 %all-to-all-start = ((bf16[64,16,128]{2,1,0:T(8,128)(2,1)}), bf16[64,16,128]{2,1,0:T(8,128)(2,1)S(1)}, u32[]{:S(2)}, u32[]{:S(2)}) async-start(bf16[64,16,128]{2,1,0:T(8,128)(2,1)} %time_sum.1), calls=%async_computation | async-start | bytes 524288 | tf_op jit(solution)/shard_map/all_to_all | solution.py:292
  15.6 0.0 copy-done
  15.7 1.9 %side.1 = (f32[1,256]{1,0:T(1,128)S(1)}, bf16[2,1024,256]{2,1,0:T(8,128)(2,1)S(1)}, bf16[2,1024,256]{2,1,0:T(8,128)(2,1)S(1)}, bf16[2,1024,256]{2,1,0:T(8,128)(2,1)S(1)}) custom-call(s32[1]{0:T(128)} %bitcast.3.refs_0_, s32[32,128]{1,0:T(8,128)S(1)} %bitcast.7, bf16[4,2,2,1024,256]{4,3,2,1,0:T(8,128)(2,1)} %refs_2_.3), custom_call_target="tpu_custom_call" | custom-call | flops 10000000 | bytes 8388608 | tf_op jit(solution)/shard_map/side/pallas_call | solution.py:297
  17.6 10.1 %all-to-all-done.refs_0_ = bf16[64,16,128]{2,1,0:T(8,128)(2,1)S(1)} async-done(((bf16[64,16,128]{2,1,0:T(8,128)(2,1)}), bf16[64,16,128]{2,1,0:T(8,128)(2,1)S(1)}, u32[]{:S(2)}, u32[]{:S(2)}) %all-to-all-start) | async-done | bytes 262176 | tf_op jit(solution)/shard_map/all_to_all | solution.py:292
  27.6 3.0 %beam.1 = (f32[16,1024]{1,0:T(8,128)S(1)}, bf16[16,1024]{1,0:T(8,128)(2,1)S(1)}) custom-call(bf16[64,16,128]{2,1,0:T(8,128)(2,1)S(1)} %all-to-all-done.refs_0_, f32[1,256]{1,0:T(1,128)S(1)} %get-tuple-element.17.refs_1_, bf16[4,2,2,1024,256]{4,3,2,1,0:T(8,128)(2,1)} %refs_2_.3, bf16[2,1024,256]{2,1,0:T(8,128)(2,1)S(1)} %get-tuple-element.18.refs_3_, ...), custom_call_target="tpu_custom_call" | custom-call | tf_op jit(solution)/shard_map/beam/pallas_call | solution.py:313
  30.7 1.4 %collective-permute-start.1 = (bf16[16,1024]{1,0:T(8,128)(2,1)S(1)}, bf16[16,1024]{1,0:T(8,128)(2,1)S(1)}, u32[]{:S(2)}, u32[]{:S(2)}) collective-permute-start(bf16[16,1024]{1,0:T(8,128)(2,1)S(1)} %get-tuple-element.22), channel_id=1, source_target_pairs={{0,1},{1,2},{2,3},{3,0},{4,5},{5,6},{6,7},{7,4},{8,9},{9,10},{10,1... | collective-permute-start | bytes 98312 | tf_op jit(solution)/shard_map/ppermute | solution.py:342
  32.0 2.6 %collective-permute-start.2 = (bf16[16,1024]{1,0:T(8,128)(2,1)S(1)}, bf16[16,1024]{1,0:T(8,128)(2,1)S(1)}, u32[]{:S(2)}, u32[]{:S(2)}) collective-permute-start(bf16[16,1024]{1,0:T(8,128)(2,1)S(1)} %get-tuple-element.22), channel_id=1, source_target_pairs={{0,2},{1,3},{2,0},{3,1},{4,6},{5,7},{6,4},{7,5},{8,10},{9,11},{10,... | collective-permute-start | bytes 98312 | tf_op jit(solution)/shard_map/ppermute | solution.py:342
  34.7 1.1 %collective-permute-start.3 = (bf16[16,1024]{1,0:T(8,128)(2,1)S(1)}, bf16[16,1024]{1,0:T(8,128)(2,1)S(1)}, u32[]{:S(2)}, u32[]{:S(2)}) collective-permute-start(bf16[16,1024]{1,0:T(8,128)(2,1)S(1)} %get-tuple-element.22), channel_id=1, source_target_pairs={{0,3},{1,0},{2,1},{3,2},{4,7},{5,4},{6,5},{7,6},{8,11},{9,8},{10,9... | collective-permute-start | bytes 98312 | tf_op jit(solution)/shard_map/ppermute | solution.py:342
  35.7 1.6 %legendre_fetch.1.refs_5_ = bf16[4,1024,256]{2,1,0:T(8,128)(2,1)S(1)} custom-call(f32[16,1024]{1,0:T(8,128)S(1)} %get-tuple-element.21.after_ref.refs_1_, bf16[4,1024,256]{2,1,0:T(8,128)(2,1)} %table_ref.2), custom_call_target="tpu_custom_call" | custom-call | bytes 4200000 | tf_op jit(solution)/shard_map/legendre_fetch/pallas_call | solution.py:345
  37.3 0.0 copy-start.2
  37.4 0.0 collective-permute-done.1.refs_2_
  37.4 0.0 collective-permute-done.2.refs_3_
  37.4 0.3 collective-permute-done.3.refs_4_
  37.7 0.0 copy-done.1
  37.7 1.8 %legendre.1 = f32[64,1,64]{2,1,0:T(1,128)} custom-call(s32[4]{0:T(128)S(1)} %copy-done.1, f32[16,1024]{1,0:T(8,128)S(1)} %get-tuple-element.21.after_ref.refs_1_, bf16[16,1024]{1,0:T(8,128)(2,1)S(1)} %collective-permute-done.1.refs_2_, bf16[16,1024]{1,0:T(8,128)(2,1)S(1)} %collective-permute-done.2.refs_3_, ...), custom_call_target="tpu_custom_call" | custom-call | tf_op jit(solution)/shard_map/legendre/pallas_call | solution.py:355
  39.5 7.4 %all-to-all-start.1 = ((f32[64,1,64]{2,1,0:T(1,128)}), f32[64,1,64]{2,1,0:T(1,128)S(1)}, u32[]{:S(2)}, u32[]{:S(2)}) async-start(f32[64,1,64]{2,1,0:T(1,128)} %legendre.1), calls=%async_computation.1 | async-start | bytes 65536 | tf_op jit(solution)/shard_map/all_to_all | solution.py:370
  47.0 0.0 copy-done.2
  47.0 1.5 %circle_tables.1 = (f32[4,2,16,256]{3,2,1,0:T(8,128)S(1)}, bf16[4,512,256]{2,1,0:T(8,128)(2,1)S(1)}) custom-call(s32[4]{0:T(128)S(1)} %copy-done.2), custom_call_target="tpu_custom_call" | custom-call | flops 10000000 | bytes 1200000 | tf_op jit(solution)/shard_map/circle_tables/pallas_call | solution.py:329
  48.5 7.7 %all-to-all-done.1.refs_1_ = f32[64,1,64]{2,1,0:T(1,128)S(1)} async-done(((f32[64,1,64]{2,1,0:T(1,128)}), f32[64,1,64]{2,1,0:T(1,128)S(1)}, u32[]{:S(2)}, u32[]{:S(2)}) %all-to-all-start.1) | async-done | bytes 16416 | tf_op jit(solution)/shard_map/all_to_all | solution.py:370
  56.2 1.6 %synthesis.1 = f32[2,4,2048]{2,1,0:T(4,128)} custom-call(s32[4]{0:T(128)S(1)} %copy-done.2, f32[64,1,64]{2,1,0:T(1,128)S(1)} %all-to-all-done.1.refs_1_, f32[4,2,16,256]{3,2,1,0:T(8,128)S(1)} %get-tuple-element.23.refs_2_, bf16[4,512,256]{2,1,0:T(8,128)(2,1)S(1)} %get-tuple-element.24.refs_3_), custom_call_target="tpu_custom_call" | custom-call | tf_op jit(solution)/shard_map/synthesis/pallas_call | solution.py:371
  (3 shorter events, 0.0 us)
Async XLA Ops:
  0.0 15.6 %copy-start = (s32[4096,1]{0,1:T(1,128)S(1)}, s32[4096,1]{0,1:T(1,128)}, u32[]{:S(2)}) copy-start(s32[4096,1]{0,1:T(1,128)} %param.8) | copy-start | bytes 49156
  0.0 4.5 %collective-permute-start = (bf16[32,2,2,256]{3,2,1,0:T(2,128)(2,1)}, bf16[32,2,2,256]{3,2,1,0:T(2,128)(2,1)S(1)}, u32[]{:S(2)}, u32[]{:S(2)}) collective-permute-start(bf16[32,2,2,256]{3,2,1,0:T(2,128)(2,1)} %signal_ref.1), channel_id=1, source_target_pairs={{0,4},{4,0},{8,12},{12,8},{16,20},{20,16},{24,28},{28,24},{32,36},... | collective-permute-start | bytes 196616 | tf_op jit(solution)/shard_map/ppermute | solution.py:265
  5.7 21.9 %all-to-all-start = ((bf16[64,16,128]{2,1,0:T(8,128)(2,1)}), bf16[64,16,128]{2,1,0:T(8,128)(2,1)S(1)}, u32[]{:S(2)}, u32[]{:S(2)}) async-start(bf16[64,16,128]{2,1,0:T(8,128)(2,1)} %time_sum.1), calls=%async_computation | async-start | bytes 524288 | tf_op jit(solution)/shard_map/all_to_all | solution.py:292
  30.7 6.7 %collective-permute-start.1 = (bf16[16,1024]{1,0:T(8,128)(2,1)S(1)}, bf16[16,1024]{1,0:T(8,128)(2,1)S(1)}, u32[]{:S(2)}, u32[]{:S(2)}) collective-permute-start(bf16[16,1024]{1,0:T(8,128)(2,1)S(1)} %get-tuple-element.22), channel_id=1, source_target_pairs={{0,1},{1,2},{2,3},{3,0},{4,5},{5,6},{6,7},{7,4},{8,9},{9,10},{10,1... | collective-permute-start | bytes 98312 | tf_op jit(solution)/shard_map/ppermute | solution.py:342
  32.0 5.3 %collective-permute-start.2 = (bf16[16,1024]{1,0:T(8,128)(2,1)S(1)}, bf16[16,1024]{1,0:T(8,128)(2,1)S(1)}, u32[]{:S(2)}, u32[]{:S(2)}) collective-permute-start(bf16[16,1024]{1,0:T(8,128)(2,1)S(1)} %get-tuple-element.22), channel_id=1, source_target_pairs={{0,2},{1,3},{2,0},{3,1},{4,6},{5,7},{6,4},{7,5},{8,10},{9,11},{10,... | collective-permute-start | bytes 98312 | tf_op jit(solution)/shard_map/ppermute | solution.py:342
  34.7 3.1 %collective-permute-start.3 = (bf16[16,1024]{1,0:T(8,128)(2,1)S(1)}, bf16[16,1024]{1,0:T(8,128)(2,1)S(1)}, u32[]{:S(2)}, u32[]{:S(2)}) collective-permute-start(bf16[16,1024]{1,0:T(8,128)(2,1)S(1)} %get-tuple-element.22), channel_id=1, source_target_pairs={{0,3},{1,0},{2,1},{3,2},{4,7},{5,4},{6,5},{7,6},{8,11},{9,8},{10,9... | collective-permute-start | bytes 98312 | tf_op jit(solution)/shard_map/ppermute | solution.py:342
  35.7 2.0 %copy-start.1 = (s32[4]{0:T(128)S(1)}, s32[4]{0:T(128)}, u32[]{:S(2)}) copy-start(s32[4]{0:T(128)} %refs_0_.3) | copy-start | bytes 52
  37.3 9.6 %copy-start.2 = (s32[4]{0:T(128)S(1)}, s32[4]{0:T(128)}, u32[]{:S(2)}) copy-start(s32[4]{0:T(128)} %refs_0_.5) | copy-start | bytes 52
  39.5 16.7 %all-to-all-start.1 = ((f32[64,1,64]{2,1,0:T(1,128)}), f32[64,1,64]{2,1,0:T(1,128)S(1)}, u32[]{:S(2)}, u32[]{:S(2)}) async-start(f32[64,1,64]{2,1,0:T(1,128)} %legendre.1), calls=%async_computation.1 | async-start | bytes 65536 | tf_op jit(solution)/shard_map/all_to_all | solution.py:370

commit v2 on v1

--- a/solution.py
+++ b/solution.py
@@ -163,13 +163,6 @@
     send_ref[...] = total.astype(BF16)
 
 
-def legendre_fetch_kernel(after_ref, table_ref, near_ref, semaphore):
-    del after_ref
-    copy = pltpu.make_async_copy(table_ref, near_ref, semaphore)
-    copy.start()
-    copy.wait()
-
-
 def legendre_kernel(
     nfreq, rows_ref, own_ref, first_ref, second_ref, third_ref, table_ref, out_ref, scratch_ref
 ):
@@ -205,14 +198,35 @@
         outer_ref[circle, 0], outer_ref[circle, 1] = cos_sin(
             (mode * step).astype(F32), period, inverse
         )
-        mode = mode_of(iota((modes, INNER), 0), modes, mode_dev)
-        step = iota((modes, INNER), 1) * 2 + 1
+        blocks = modes // mode_dev
+        mode = iota((blocks, INNER), 0) * mode_dev
+        step = iota((blocks, INNER), 1) * 2 + 1
         cosine, sine = cos_sin((mode * step).astype(F32), period, inverse)
-        factor = jnp.where(mode == 0, 1.0, 2.0)
-        for part, value in enumerate((cosine * factor, -sine * factor)):
-            high, low = split(value)
-            inner_ref[circle, part * modes : (part + 1) * modes, :INNER] = high
-            inner_ref[circle, part * modes : (part + 1) * modes, INNER:] = low
+        first = jnp.where(mode == 0, 1.0, 2.0)
+        small = (8, INNER)
+        small_step = (iota(small, 0) * (iota(small, 1) * 2 + 1)).astype(F32)
+        turn_cosine, turn_sine = cos_sin(small_step, period, inverse)
+        for j in range(mode_dev):
+            c, s = turn_cosine[j : j + 1], turn_sine[j : j + 1]
+            factor = first if j == 0 else 2.0
+            for part, value in enumerate(
+                ((cosine * c - sine * s) * factor, (sine * c + cosine * s) * -factor)
+            ):
+                high, low = split(value)
+                at = part * modes + j * blocks
+                inner_ref[circle, at : at + blocks, :INNER] = high
+                inner_ref[circle, at : at + blocks, INNER:] = low
+
+
+def middle_kernel(
+    modes, mode_dev, count_ref, after_ref, legendre_ref,
+    near_ref, outer_ref, inner_ref, semaphore,
+):
+    del after_ref
+    copy = pltpu.make_async_copy(legendre_ref, near_ref, semaphore)
+    copy.start()
+    table_kernel(modes, mode_dev, count_ref, outer_ref, inner_ref)
+    copy.wait()
 
 
 def synthesis_kernel(nfreq, count_ref, value_ref, outer_ref, inner_ref, map_ref):
@@ -326,32 +340,26 @@
         far_beam,
         *(pltpu.with_memory_space_constraint(a, pltpu.VMEM) for a in near_blocks),
     )
-    outer, inner = pl.pallas_call(
-        lambda *refs: table_kernel(modes, mode_dev, *refs),
-        out_shape=(
-            pltpu.VMEM((circles, 2, OUTER, modes), F32),
-            pltpu.VMEM((circles, 2 * modes, 2 * INNER), BF16),
-        ),
-        in_specs=[SMEM],
-        out_specs=(VMEM, VMEM),
-        compiler_params=PARAMS,
-        cost_estimate=pl.CostEstimate(flops=10000000, bytes_accessed=1200000, transcendentals=0),
-        name="circle_tables",
-    )(circle_pixels)
     arrived = [
         lax.ppermute(send, "freq", [(i, (i + k) % freq_count) for i in range(freq_count)])
         for k in range(1, freq_count)
     ]
-    near_legendre = pl.pallas_call(
-        legendre_fetch_kernel,
-        out_shape=(pltpu.VMEM(legendre.shape, BF16),),
-        in_specs=[ANY, ANY],
-        out_specs=(VMEM,),
+    near_legendre, outer, inner = pl.pallas_call(
+        lambda *refs: middle_kernel(modes, mode_dev, *refs),
+        out_shape=(
+            pltpu.VMEM(legendre.shape, BF16),
+            pltpu.VMEM((circles, 2, OUTER, modes), F32),
+            pltpu.VMEM((circles, 2 * modes, 2 * INNER), BF16),
+        ),
+        in_specs=[SMEM, ANY, ANY],
+        out_specs=(VMEM,) * 3,
         scratch_shapes=[pltpu.SemaphoreType.DMA(())],
         compiler_params=PARAMS,
-        cost_estimate=pl.CostEstimate(flops=0, bytes_accessed=4200000, transcendentals=0),
-        name="legendre_fetch",
-    )(own, pltpu.with_memory_space_constraint(legendre, pltpu.HBM))[0]
+        cost_estimate=pl.CostEstimate(
+            flops=10000000, bytes_accessed=4200000, transcendentals=0
+        ),
+        name="middle",
+    )(circle_pixels, own, pltpu.with_memory_space_constraint(legendre, pltpu.HBM))
     latitude = pl.pallas_call(
         lambda *refs: legendre_kernel(nfreq, *refs),
         out_shape=(pltpu.VMEM((ma_count, 1, circles * rows), F32),),

time: 58 us -> 57.7 us (level)
  blocking collectives: 0 us -> 16.5 us
  starting transfers between devices: 25.7 us -> 17 us
  waiting for transfers between devices: 18.1 us -> 11.5 us
  Pallas kernels: 13.8 us -> 12.2 us
    all_to_all x0 -> x1, blocking collectives: none -> 16.5 us  [body(): regrouped = lax.all_to_all(latitude, 'ma', 0, 0)]
    all_to_all x1 -> x0, waiting for transfers between devices: 7.71 us -> none  [body(): regrouped = lax.all_to_all(latitude, 'ma', 0, 0)]
    all_to_all x1 -> x0, starting transfers between devices: 7.44 us -> none  [body(): regrouped = lax.all_to_all(latitude, 'ma', 0, 0)]
    ppermute x3, starting transfers between devices: 5.06 us -> 3.85 us  [body(): lax.ppermute(send, 'freq', [(i, (i + k) % freq_count) for i in range(freq...]
    ppermute x3, waiting for transfers between devices: 0.34 us -> 1.42 us  [body(): lax.ppermute(send, 'freq', [(i, (i + k) % freq_count) for i in range(freq...]
    pallas_call x2 -> x1, Pallas kernels: 3.09 us -> 2.14 us  [body(): pl.pallas_call(lambda *refs: middle_kernel(modes, mode_dev, *refs), out_s...]
    pallas_call x1, Pallas kernels: 1.8 us -> 1.18 us  [body(): pl.pallas_call(lambda *refs: legendre_kernel(nfreq, *refs), out_shape=(pl...]
  transfers between devices with their start and end apart: 6 -> 5, of which waited for: 3 -> 3; matrix products, arithmetic and copies ran while one was open for 0% -> 0% of each run, Pallas kernels for 11% -> 9%
where the time goes in v2:
time: 57.7 us; the launch traced here: 57.4 us
  starting transfers between devices  17 us (29%)
  blocking collectives  16.5 us (29%)
  Pallas kernels  12.2 us (21%)
  waiting for transfers between devices  11.5 us (20%)
    all_to_all x1, blocking collectives, body(): regrouped = lax.all_to_all(latitude, 'ma', 0, 0)  16.5 us
    all_to_all x1, waiting for transfers between devices, body(): received = lax.all_to_all(partial_spectrum, 'ma', 0, 0)  10.1 us
    all_to_all x1, starting transfers between devices, body(): received = lax.all_to_all(partial_spectrum, 'ma', 0, 0)  9.92 us
    ppermute x3, starting transfers between devices, body(): lax.ppermute(send, 'freq', [(i, (i + k) % freq_count) for i in range(freq...  3.85 us
    ppermute x1, starting transfers between devices, body(): lax.ppermute(visibility, 'ma', [(i, i ^ 1) for i in range(ma_count)])  3.24 us
    pallas_call x1, Pallas kernels, body(): pl.pallas_call(lambda *refs: beam_kernel(nfreq, *refs), out_shape=(pltpu....  3.02 us
    pallas_call x1, Pallas kernels, body(): pl.pallas_call(lambda *refs: middle_kernel(modes, mode_dev, *refs), out_s...  2.14 us
    pallas_call x1, Pallas kernels, body(): pl.pallas_call(lambda *refs: side_kernel(nfreq, *refs), out_shape=(pltpu....  1.89 us
  transfers between devices with their start and end apart: 5, of which 3 were waited for; matrix products, arithmetic and copies ran while one was open for 0% of the time, Pallas kernels for 9%

profile of v2, /device:TPU:1, one launch (start us, length us, event | category | flops | bytes accessed | tf_op | source)
XLA Modules:
  0.0 57.4 jit_solution(1845679447404725456)
XLA Ops:
  0.0 0.0 copy-start
  0.0 3.2 %collective-permute-start = (bf16[32,2,2,256]{3,2,1,0:T(2,128)(2,1)}, bf16[32,2,2,256]{3,2,1,0:T(2,128)(2,1)S(1)}, u32[]{:S(2)}, u32[]{:S(2)}) collective-permute-start(bf16[32,2,2,256]{3,2,1,0:T(2,128)(2,1)} %signal_ref.1), channel_id=1, source_target_pairs={{0,4},{4,0},{8,12},{12,8},{16,20},{20,16},{24,28},{28,24},{32,36},... | collective-permute-start | bytes 196616 | tf_op jit(solution)/shard_map/ppermute | solution.py:279
  3.2 1.3 %fetch.1 = (bf16[2,1024,256]{2,1,0:T(8,128)(2,1)S(1)}, bf16[32,2,2,128]{3,2,1,0:T(2,128)(2,1)S(1)}) custom-call(s32[1]{0:T(128)} %bitcast.place_ref.refs_0_, bf16[2,1024,256]{2,1,0:T(8,128)(2,1)} %constant.29.clone.table_ref, bf16[32,2,2,256]{3,2,1,0:T(2,128)(2,1)} %signal_ref.1), custom_call_target="tpu_custom_call" | custom-call | bytes 2200000 | tf_op jit(solution)/shard_map/fetch/pallas_call | solution.py:282
  4.5 0.0 collective-permute-done
  4.6 1.2 %time_sum.1 = bf16[64,16,128]{2,1,0:T(8,128)(2,1)} custom-call(s32[1]{0:T(128)} %bitcast.place_ref.refs_0_, bf16[2,1024,256]{2,1,0:T(8,128)(2,1)S(1)} %get-tuple-element.16.refs_1_, bf16[128,128]{1,0:T(8,128)(2,1)S(1)} %bitcast.6, bf16[128,128]{1,0:T(8,128)(2,1)S(1)} %bitcast.5), custom_call_target="tpu_custom_call" | custom-call | tf_op jit(solution)/shard_map/time_sum/pallas_call | solution.py:64
  5.7 9.9 %all-to-all-start = ((bf16[64,16,128]{2,1,0:T(8,128)(2,1)}), bf16[64,16,128]{2,1,0:T(8,128)(2,1)S(1)}, u32[]{:S(2)}, u32[]{:S(2)}) async-start(bf16[64,16,128]{2,1,0:T(8,128)(2,1)} %time_sum.1), calls=%async_computation | async-start | bytes 524288 | tf_op jit(solution)/shard_map/all_to_all | solution.py:306
  15.6 0.0 copy-done
  15.7 1.9 %side.1 = (f32[1,256]{1,0:T(1,128)S(1)}, bf16[2,1024,256]{2,1,0:T(8,128)(2,1)S(1)}, bf16[2,1024,256]{2,1,0:T(8,128)(2,1)S(1)}, bf16[2,1024,256]{2,1,0:T(8,128)(2,1)S(1)}) custom-call(s32[1]{0:T(128)} %bitcast.3.refs_0_, s32[32,128]{1,0:T(8,128)S(1)} %bitcast.7, bf16[4,2,2,1024,256]{4,3,2,1,0:T(8,128)(2,1)} %refs_2_.4), custom_call_target="tpu_custom_call" | custom-call | flops 10000000 | bytes 8388608 | tf_op jit(solution)/shard_map/side/pallas_call | solution.py:311
  17.6 10.1 %all-to-all-done.refs_0_ = bf16[64,16,128]{2,1,0:T(8,128)(2,1)S(1)} async-done(((bf16[64,16,128]{2,1,0:T(8,128)(2,1)}), bf16[64,16,128]{2,1,0:T(8,128)(2,1)S(1)}, u32[]{:S(2)}, u32[]{:S(2)}) %all-to-all-start) | async-done | bytes 262176 | tf_op jit(solution)/shard_map/all_to_all | solution.py:306
  27.6 0.0 copy-start.1
  27.6 3.0 %beam.1 = (f32[16,1024]{1,0:T(8,128)S(1)}, bf16[16,1024]{1,0:T(8,128)(2,1)S(1)}) custom-call(bf16[64,16,128]{2,1,0:T(8,128)(2,1)S(1)} %all-to-all-done.refs_0_, f32[1,256]{1,0:T(1,128)S(1)} %get-tuple-element.18.refs_1_, bf16[4,2,2,1024,256]{4,3,2,1,0:T(8,128)(2,1)} %refs_2_.4, bf16[2,1024,256]{2,1,0:T(8,128)(2,1)S(1)} %get-tuple-element.19.refs_3_, ...), custom_call_target="tpu_custom_call" | custom-call | tf_op jit(solution)/shard_map/beam/pallas_call | solution.py:327
  30.7 0.0 copy-start.2
  30.7 2.8 %collective-permute-start.3 = (bf16[16,1024]{1,0:T(8,128)(2,1)S(1)}, bf16[16,1024]{1,0:T(8,128)(2,1)S(1)}, u32[]{:S(2)}, u32[]{:S(2)}) collective-permute-start(bf16[16,1024]{1,0:T(8,128)(2,1)S(1)} %get-tuple-element.23), channel_id=1, source_target_pairs={{0,3},{1,0},{2,1},{3,2},{4,7},{5,4},{6,5},{7,6},{8,11},{9,8},{10,9... | collective-permute-start | bytes 98312 | tf_op jit(solution)/shard_map/ppermute | solution.py:344
  33.5 0.3 collective-permute-start.2
  33.8 0.7 %collective-permute-start.1 = (bf16[16,1024]{1,0:T(8,128)(2,1)S(1)}, bf16[16,1024]{1,0:T(8,128)(2,1)S(1)}, u32[]{:S(2)}, u32[]{:S(2)}) collective-permute-start(bf16[16,1024]{1,0:T(8,128)(2,1)S(1)} %get-tuple-element.23), channel_id=1, source_target_pairs={{0,1},{1,2},{2,3},{3,0},{4,5},{5,6},{6,7},{7,4},{8,9},{9,10},{10,1... | collective-permute-start | bytes 98312 | tf_op jit(solution)/shard_map/ppermute | solution.py:344
  34.5 0.0 copy-done.1
  34.5 2.1 %middle.1 = (bf16[4,1024,256]{2,1,0:T(8,128)(2,1)S(1)}, f32[4,2,16,256]{3,2,1,0:T(8,128)S(1)}, bf16[4,512,256]{2,1,0:T(8,128)(2,1)S(1)}) custom-call(s32[4]{0:T(128)S(1)} %copy-done.1, f32[16,1024]{1,0:T(8,128)S(1)} %get-tuple-element.22.refs_1_, bf16[4,1024,256]{2,1,0:T(8,128)(2,1)} %refs_2_.5), custom_call_target="tpu_custom_call" | custom-call | flops 10000000 | bytes 4200000 | tf_op jit(solution)/shard_map/middle/pallas_call | solution.py:347
  36.7 0.0 collective-permute-done.3.refs_4_
  36.7 1.1 %collective-permute-done.2.refs_3_ = bf16[16,1024]{1,0:T(8,128)(2,1)S(1)} collective-permute-done((bf16[16,1024]{1,0:T(8,128)(2,1)S(1)}, bf16[16,1024]{1,0:T(8,128)(2,1)S(1)}, u32[]{:S(2)}, u32[]{:S(2)}) %collective-permute-start.2) | collective-permute-done | bytes 32800 | tf_op jit(solution)/shard_map/ppermute | solution.py:344
  37.8 0.3 collective-permute-done.1.refs_2_
  38.1 0.0 copy-done.2
  38.1 1.2 %legendre.1 = f32[64,1,64]{2,1,0:T(1,128)S(1)} custom-call(s32[4]{0:T(128)S(1)} %copy-done.2, f32[16,1024]{1,0:T(8,128)S(1)} %get-tuple-element.22.refs_1_, bf16[16,1024]{1,0:T(8,128)(2,1)S(1)} %collective-permute-done.1.refs_2_, bf16[16,1024]{1,0:T(8,128)(2,1)S(1)} %collective-permute-done.2.refs_3_, bf16[16,1024]{1,0:T(8,128)(2,1)S(1)} %collective-permute-done.3.refs_4_, ...), custom_call_target="tpu_custom_call" | custom-call | tf_op jit(solution)/shard_map/legendre/pallas_call | solution.py:363
  39.3 16.5 %all_to_all.10.refs_1_ = f32[64,1,64]{2,1,0:T(1,128)S(1)} all-to-all(f32[64,1,64]{2,1,0:T(1,128)S(1)} %legendre.1), channel_id=1, replica_groups=mesh['ma'=64,'freq'=4] {'ma'}, dimensions={0} | all-to-all | bytes 32768 | tf_op jit(solution)/shard_map/all_to_all | solution.py:378
  55.8 1.6 %synthesis.1 = f32[2,4,2048]{2,1,0:T(4,128)} custom-call(s32[4]{0:T(128)S(1)} %copy-done.1, f32[64,1,64]{2,1,0:T(1,128)S(1)} %all_to_all.10.refs_1_, f32[4,2,16,256]{3,2,1,0:T(8,128)S(1)} %get-tuple-element.25.refs_2_, bf16[4,512,256]{2,1,0:T(8,128)(2,1)S(1)} %get-tuple-element.26.refs_3_), custom_call_target="tpu_custom_call" | custom-call | tf_op jit(solution)/shard_map/synthesis/pallas_call | solution.py:379
  (1 shorter events, 0.0 us)
Async XLA Ops:
  0.0 15.6 %copy-start = (s32[4096,1]{0,1:T(1,128)S(1)}, s32[4096,1]{0,1:T(1,128)}, u32[]{:S(2)}) copy-start(s32[4096,1]{0,1:T(1,128)} %param.8) | copy-start | bytes 49156
  0.0 4.5 %collective-permute-start = (bf16[32,2,2,256]{3,2,1,0:T(2,128)(2,1)}, bf16[32,2,2,256]{3,2,1,0:T(2,128)(2,1)S(1)}, u32[]{:S(2)}, u32[]{:S(2)}) collective-permute-start(bf16[32,2,2,256]{3,2,1,0:T(2,128)(2,1)} %signal_ref.1), channel_id=1, source_target_pairs={{0,4},{4,0},{8,12},{12,8},{16,20},{20,16},{24,28},{28,24},{32,36},... | collective-permute-start | bytes 196616 | tf_op jit(solution)/shard_map/ppermute | solution.py:279
  5.7 21.9 %all-to-all-start = ((bf16[64,16,128]{2,1,0:T(8,128)(2,1)}), bf16[64,16,128]{2,1,0:T(8,128)(2,1)S(1)}, u32[]{:S(2)}, u32[]{:S(2)}) async-start(bf16[64,16,128]{2,1,0:T(8,128)(2,1)} %time_sum.1), calls=%async_computation | async-start | bytes 524288 | tf_op jit(solution)/shard_map/all_to_all | solution.py:306
  27.6 6.9 %copy-start.1 = (s32[4]{0:T(128)S(1)}, s32[4]{0:T(128)}, u32[]{:S(2)}) copy-start(s32[4]{0:T(128)} %refs_0_.5) | copy-start | bytes 52
  30.7 7.4 %copy-start.2 = (s32[4]{0:T(128)S(1)}, s32[4]{0:T(128)}, u32[]{:S(2)}) copy-start(s32[4]{0:T(128)} %refs_0_.4) | copy-start | bytes 52
  30.7 6.0 %collective-permute-start.3 = (bf16[16,1024]{1,0:T(8,128)(2,1)S(1)}, bf16[16,1024]{1,0:T(8,128)(2,1)S(1)}, u32[]{:S(2)}, u32[]{:S(2)}) collective-permute-start(bf16[16,1024]{1,0:T(8,128)(2,1)S(1)} %get-tuple-element.23), channel_id=1, source_target_pairs={{0,3},{1,0},{2,1},{3,2},{4,7},{5,4},{6,5},{7,6},{8,11},{9,8},{10,9... | collective-permute-start | bytes 98312 | tf_op jit(solution)/shard_map/ppermute | solution.py:344
  33.5 4.3 %collective-permute-start.2 = (bf16[16,1024]{1,0:T(8,128)(2,1)S(1)}, bf16[16,1024]{1,0:T(8,128)(2,1)S(1)}, u32[]{:S(2)}, u32[]{:S(2)}) collective-permute-start(bf16[16,1024]{1,0:T(8,128)(2,1)S(1)} %get-tuple-element.23), channel_id=1, source_target_pairs={{0,2},{1,3},{2,0},{3,1},{4,6},{5,7},{6,4},{7,5},{8,10},{9,11},{10,... | collective-permute-start | bytes 98312 | tf_op jit(solution)/shard_map/ppermute | solution.py:344
  33.8 4.3 %collective-permute-start.1 = (bf16[16,1024]{1,0:T(8,128)(2,1)S(1)}, bf16[16,1024]{1,0:T(8,128)(2,1)S(1)}, u32[]{:S(2)}, u32[]{:S(2)}) collective-permute-start(bf16[16,1024]{1,0:T(8,128)(2,1)S(1)} %get-tuple-element.23), channel_id=1, source_target_pairs={{0,1},{1,2},{2,3},{3,0},{4,5},{5,6},{6,7},{7,4},{8,9},{9,10},{10,1... | collective-permute-start | bytes 98312 | tf_op jit(solution)/shard_map/ppermute | solution.py:344

commit v3 on v2

--- a/solution.py
+++ b/solution.py
@@ -71,26 +71,36 @@
     )(*args)
 
 
-def phase_table(modes, nfreq, chip_times, ntime):
-    row = np.arange(2 * modes * nfreq)[:, None]
+def phase_table(modes, mode_dev, nfreq, chip_times, ntime):
+    half = modes // 2
+    row = np.arange(2 * half * nfreq)[:, None]
     column = np.arange(chip_times * 2 * nfreq)[None, :]
-    part_out, mode, freq_out = row // (modes * nfreq), row // nfreq % modes, row % nfreq
+    part_out, place, freq_out = row // (half * nfreq), row // nfreq % half, row % nfreq
     time, part_in, freq_in = column // (2 * nfreq), column // nfreq % 2, column % nfreq
-    phase = (mode * time + (part_out - part_in) * (ntime // 4)) % ntime
-    value = np.cos(phase * (2.0 * math.pi / ntime)) / math.sqrt(ntime) * (freq_out == freq_in)
-    high = value.astype(ml_dtypes.bfloat16)
-    low = (value - high.astype(np.float64)).astype(ml_dtypes.bfloat16)
-    return np.stack([high, low])
-
-
-def fetch_kernel(place_ref, table_ref, signal_ref, near_ref, own_ref, semaphores):
-    width = own_ref.shape[3]
-    start = pl.multiple_of(place_ref[0] % 2 * width, width)
+    tables = []
+    for core in range(2):
+        mode = place // mode_dev * (2 * mode_dev) + core * mode_dev + place % mode_dev
+        phase = (mode * time + (part_out - part_in) * (ntime // 4)) % ntime
+        value = np.cos(phase * (2.0 * math.pi / ntime)) / math.sqrt(ntime)
+        value = value * (freq_out == freq_in)
+        high = value.astype(ml_dtypes.bfloat16)
+        low = (value - high.astype(np.float64)).astype(ml_dtypes.bfloat16)
+        tables.append(np.stack([high, low]))
+    return np.stack(tables)
+
+
+def fetch_kernel(table_ref, signal_ref, near_ref, left_ref, right_ref, semaphores):
+    width = left_ref.shape[3]
     copies = [
         pltpu.make_async_copy(
-            signal_ref.at[:, :, :, pl.ds(start, width)], own_ref, semaphores.at[0]
-        ),
-        pltpu.make_async_copy(table_ref, near_ref, semaphores.at[1]),
+            signal_ref.at[:, :, :, :width], left_ref, semaphores.at[0]
+        ),
+        pltpu.make_async_copy(
+            signal_ref.at[:, :, :, width:], right_ref, semaphores.at[1]
+        ),
+        pltpu.make_async_copy(
+            table_ref.at[lax.rem(lax.axis_index("ma"), 2)], near_ref, semaphores.at[2]
+        ),
     ]
     for copy in copies:
         copy.start()
@@ -98,27 +108,35 @@
         copy.wait()
 
 
-def time_kernel(nfreq, chips, place_ref, table_ref, own_ref, other_ref, out_ref):
-    even = place_ref[0] % 2 == 0
-    own, other = own_ref[...], other_ref[...]
+def time_kernel(nfreq, chips, mode_dev, table_ref, *refs):
+    *signal_refs, out_ref = refs
+    place = lax.axis_index("ma")
+    core = lax.rem(place, 2)
+    own_left, own_right, other_left, other_right = (ref[...] for ref in signal_refs)
+    own = jnp.concatenate([own_left, own_right], 1)
+    other = jnp.concatenate([other_left, other_right], 1)
+    even = core == 0
     signal = jnp.concatenate([jnp.where(even, own, other), jnp.where(even, other, own)], 0)
     total = dot(table_ref[0], signal, (1, 0)) + dot(table_ref[1], signal, (1, 0))
-    sources, rows, width = out_ref.shape
-    phase = iota((chips * nfreq, width), 0) // nfreq * (place_ref[0] // 2)
+    dests, rows, width = out_ref.shape
+    period = chips // 2 * nfreq
+    index = iota((period, width), 0) // nfreq
+    mode = index // mode_dev * (2 * mode_dev) + core * mode_dev + index % mode_dev
+    phase = mode * lax.div(place, 2)
     turn = ((phase + chips // 2) % chips - chips // 2).astype(F32) * (1.0 / chips)
     square = turn * turn
     cosine, sine = polynomial(square, COS)[None], (polynomial(square, SIN) * turn)[None]
-    real, imag = total.reshape(2, -1, chips * nfreq, width)
-    shape = (sources, rows // 2, width)
+    real, imag = total.reshape(2, -1, period, width)
+    shape = (dests, rows // 2, width)
     real, imag = real * cosine + imag * sine, imag * cosine - real * sine
     out_ref[...] = jnp.concatenate([real.reshape(shape), imag.reshape(shape)], 1).astype(BF16)
 
 
-def side_kernel(nfreq, first_ref, pair_ref, beam_ref, weight_ref, *refs):
+def side_kernel(nfreq, pair_ref, beam_ref, weight_ref, *refs):
     *block_refs, semaphores = refs
     copies = fetch_blocks(nfreq, beam_ref, 0, block_refs, semaphores)
     shape = (weight_ref.shape[1], pair_ref.shape[1])
-    ids = iota(shape, 0) + first_ref[0]
+    ids = iota(shape, 0) + lax.axis_index("freq") * shape[0]
     total = jnp.zeros(shape, F32)
     for i in range(pair_ref.shape[0]):
         total += jnp.where(pair_ref[i : i + 1, :] == ids, 1.0, 0.0)
@@ -144,10 +162,9 @@
     near = len(near_refs)
     far_refs = [far_ref.at[i] for i in range(far_ref.shape[0])]
     copies = fetch_blocks(nfreq, beam_ref, near, far_refs, semaphores)
-    sources, rows, width = part_ref.shape
+    rows = part_ref.shape[1]
     half = rows // 2
-    sums = part_ref[...].astype(F32).reshape(sources // 2, 2, rows, width).sum(0)
-    weighted = jnp.concatenate([sums[0], sums[1]], 1) * weight_ref[...]
+    weighted = part_ref[...].astype(F32).sum(0) * weight_ref[...]
     turned = jnp.concatenate([-weighted[half:], weighted[:half]], 0)
     row = iota((2 * rows, weighted.shape[1]), 0) % half
     lefts = [jnp.concatenate(split(value), 0) for value in (weighted, turned)]
@@ -177,9 +194,10 @@
     for m in range(modes):
         live = (row % modes == m) & (column < rows_ref[m])
         latitude += dot(jnp.where(live, left, jnp.zeros_like(left)), table_ref[m], (1, 0))
-    scratch_ref[...] = (latitude[:rows] + latitude[rows:]).T
+    latitude = (latitude[:rows] + latitude[rows:]).T
+    scratch_ref[: latitude.shape[0]] = latitude
     dests, _, width = out_ref.shape
-    circles = scratch_ref.shape[0] // dests
+    circles = latitude.shape[0] // dests
     pieces = [scratch_ref[pl.ds(j, dests, circles), :] for j in range(circles)]
     out_ref[...] = jnp.concatenate(pieces, 1).reshape(out_ref.shape)
 
@@ -266,8 +284,6 @@
 def body(visibility, pair_baseline, beam_inverse, block_rows, legendre, circle_pixels):
     ma_count = lax.axis_size("ma")
     freq_count = lax.axis_size("freq")
-    ma_place = lax.axis_index("ma")
-    freq_place = lax.axis_index("freq")
     time_dev, _, nfreq, base_dev = visibility.shape
     ntime = time_dev * ma_count
     mode_dev, _, _, lrows, _ = beam_inverse.shape
@@ -277,33 +293,38 @@
     rows = mode_dev * 2 * nfreq
 
     other = lax.ppermute(visibility, "ma", [(i, i ^ 1) for i in range(ma_count)])
-    other = lax.dynamic_slice_in_dim(other, ma_place % 2 * base_half, base_half, 3)
-    table = jnp.asarray(phase_table(modes, nfreq, 2 * time_dev, ntime))
-    near, own = pl.pallas_call(
+    table = jnp.asarray(phase_table(modes, mode_dev, nfreq, 2 * time_dev, ntime))
+    piece = (time_dev, 2, nfreq, base_half)
+    near, left, right = pl.pallas_call(
         fetch_kernel,
-        out_shape=(pltpu.VMEM(table.shape, BF16), pltpu.VMEM(other.shape, BF16)),
-        in_specs=[SMEM, ANY, ANY],
-        out_specs=(VMEM, VMEM),
-        scratch_shapes=[pltpu.SemaphoreType.DMA((2,))],
-        compiler_params=PARAMS,
-        cost_estimate=pl.CostEstimate(flops=0, bytes_accessed=2200000, transcendentals=0),
+        out_shape=(
+            pltpu.VMEM(table.shape[1:], BF16),
+            pltpu.VMEM(piece, BF16),
+            pltpu.VMEM(piece, BF16),
+        ),
+        in_specs=[ANY, ANY],
+        out_specs=(VMEM,) * 3,
+        scratch_shapes=[pltpu.SemaphoreType.DMA((3,))],
+        compiler_params=PARAMS,
+        cost_estimate=pl.CostEstimate(flops=0, bytes_accessed=1200000, transcendentals=0),
         name="fetch",
     )(
-        ma_place.reshape(1),
         pltpu.with_memory_space_constraint(table, pltpu.HBM),
         pltpu.with_memory_space_constraint(visibility, pltpu.HBM),
     )
     (partial_spectrum,) = call(
-        lambda *refs: time_kernel(nfreq, ma_count // 2, *refs),
-        [((ma_count, rows, base_half), BF16)],
-        [SMEM, VMEM, VMEM, VMEM],
-        ma_place.reshape(1),
+        lambda *refs: time_kernel(nfreq, ma_count // 2, mode_dev, *refs),
+        [((ma_count // 2, rows, base_dev), BF16)],
+        [VMEM] * 5,
         near,
-        own.reshape(-1, base_half),
-        other.reshape(-1, base_half),
+        *(
+            a.reshape(-1, base_half)
+            for a in (left, right, other[..., :base_half], other[..., base_half:])
+        ),
         name="time_sum",
     )
-    received = lax.all_to_all(partial_spectrum, "ma", 0, 0)
+    groups = [list(range(core, ma_count, 2)) for core in range(2)]
+    received = lax.all_to_all(partial_spectrum, "ma", 0, 0, axis_index_groups=groups)
 
     blocks = mode_dev * nfreq
     block = beam_inverse.shape[2:]
@@ -311,7 +332,7 @@
     weight, *near_blocks = pl.pallas_call(
         lambda *refs: side_kernel(nfreq, *refs),
         out_shape=(pltpu.VMEM((1, base_dev), F32),) + (pltpu.VMEM(block, BF16),) * NEAR,
-        in_specs=[SMEM, VMEM, ANY],
+        in_specs=[VMEM, ANY],
         out_specs=(VMEM,) * (1 + NEAR),
         scratch_shapes=[pltpu.SemaphoreType.DMA((NEAR,))],
         compiler_params=PARAMS,
@@ -320,7 +341,6 @@
         ),
         name="side",
     )(
-        (freq_place * base_dev).reshape(1),
         pltpu.with_memory_space_constraint(pair_baseline.reshape(-1, 128), pltpu.VMEM),
         far_beam,
     )
@@ -365,7 +385,7 @@
         out_shape=(pltpu.VMEM((ma_count, 1, circles * rows), F32),),
         in_specs=[SMEM] + [VMEM] * 5,
         out_specs=(VMEM,),
-        scratch_shapes=[pltpu.VMEM((legendre.shape[2], rows), F32)],
+        scratch_shapes=[pltpu.VMEM((legendre.shape[2] + 8, rows), F32)],
         compiler_params=PARAMS,
         name="legendre",
     )(

time: 57.7 us -> 56.8 us (0.984)
  waiting for transfers between devices: 11.5 us -> 9.19 us
  blocking collectives: 16.5 us -> 18.8 us
  starting transfers between devices: 17 us -> 16.4 us
    all_to_all x1, waiting for transfers between devices: 10.1 us -> 7.77 us  [body(): lax.all_to_all(partial_spectrum, 'ma', 0, 0, axis_index_groups=groups)]
    all_to_all x1, blocking collectives: 16.5 us -> 18.8 us  [body(): regrouped = lax.all_to_all(latitude, 'ma', 0, 0)]
    all_to_all x1, starting transfers between devices: 9.92 us -> 9.31 us  [body(): lax.all_to_all(partial_spectrum, 'ma', 0, 0, axis_index_groups=groups)]
where the time goes in v3:
time: 56.8 us; the launch traced here: 56.5 us
  blocking collectives  18.8 us (33%)
  starting transfers between devices  16.4 us (29%)
  Pallas kernels  11.9 us (21%)
  waiting for transfers between devices  9.19 us (16%)
    all_to_all x1, blocking collectives, body(): regrouped = lax.all_to_all(latitude, 'ma', 0, 0)  18.8 us
    all_to_all x1, starting transfers between devices, body(): lax.all_to_all(partial_spectrum, 'ma', 0, 0, axis_index_groups=groups)  9.31 us
    all_to_all x1, waiting for transfers between devices, body(): lax.all_to_all(partial_spectrum, 'ma', 0, 0, axis_index_groups=groups)  7.77 us
    ppermute x3, starting transfers between devices, body(): lax.ppermute(send, 'freq', [(i, (i + k) % freq_count) for i in range(freq...  3.85 us
    ppermute x1, starting transfers between devices, body(): lax.ppermute(visibility, 'ma', [(i, i ^ 1) for i in range(ma_count)])  3.24 us
    pallas_call x1, Pallas kernels, body(): pl.pallas_call(lambda *refs: beam_kernel(nfreq, *refs), out_shape=(pltpu....  3.02 us
    pallas_call x1, Pallas kernels, body(): pl.pallas_call(lambda *refs: middle_kernel(modes, mode_dev, *refs), out_s...  2.14 us
    pallas_call x1, Pallas kernels, body(): pl.pallas_call(lambda *refs: side_kernel(nfreq, *refs), out_shape=(pltpu....  1.89 us
  transfers between devices with their start and end apart: 5, of which 3 were waited for; matrix products, arithmetic and copies ran while one was open for 0% of the time, Pallas kernels for 9%

profile of v3, /device:TPU:1, one launch (start us, length us, event | category | flops | bytes accessed | tf_op | source)
XLA Modules:
  0.0 56.5 jit_solution(3051757416670341210)
XLA Ops:
  0.0 0.0 copy-start
  0.0 3.2 %collective-permute-start = (bf16[32,2,2,256]{3,2,1,0:T(2,128)(2,1)}, bf16[32,2,2,256]{3,2,1,0:T(2,128)(2,1)S(1)}, u32[]{:S(2)}, u32[]{:S(2)}) collective-permute-start(bf16[32,2,2,256]{3,2,1,0:T(2,128)(2,1)} %signal_ref.1), channel_id=1, source_target_pairs={{0,4},{4,0},{8,12},{12,8},{16,20},{20,16},{24,28},{28,24},{32,36},... | collective-permute-start | bytes 196616 | tf_op jit(solution)/shard_map/ppermute | solution.py:295
  3.2 1.1 %fetch.1 = (bf16[2,512,256]{2,1,0:T(8,128)(2,1)S(1)}, bf16[32,2,2,128]{3,2,1,0:T(2,128)(2,1)S(1)}, bf16[32,2,2,128]{3,2,1,0:T(2,128)(2,1)S(1)}) custom-call(bf16[2,2,512,256]{3,2,1,0:T(8,128)(2,1)} %constant.2.clone.table_ref, bf16[32,2,2,256]{3,2,1,0:T(2,128)(2,1)} %signal_ref.1), custom_call_target="tpu_custom_call" | custom-call | bytes 1200000 | tf_op jit(solution)/shard_map/fetch/pallas_call | solution.py:298
  4.4 0.0 collective-permute-done
  4.4 1.0 %time_sum.1 = bf16[32,16,256]{2,1,0:T(8,128)(2,1)} custom-call(bf16[2,512,256]{2,1,0:T(8,128)(2,1)S(1)} %get-tuple-element.17.refs_0_, bf16[128,128]{1,0:T(8,128)(2,1)S(1)} %bitcast.7, bf16[128,128]{1,0:T(8,128)(2,1)S(1)} %bitcast.8, bf16[128,128]{1,0:T(8,128)(2,1)S(1)} %bitcast.6, bf16[128,128]{1,0:T(8,128)(2,1)S(1)} %bitcast.5), custom_call_target="tpu_custom_call" | custom-call | tf_op jit(solution)/shard_map/time_sum/pallas_call | solution.py:64
  5.4 9.3 %all-to-all-start = ((bf16[32,16,256]{2,1,0:T(8,128)(2,1)}), bf16[32,16,256]{2,1,0:T(8,128)(2,1)S(1)}, u32[]{:S(2)}, u32[]{:S(2)}) async-start(bf16[32,16,256]{2,1,0:T(8,128)(2,1)} %time_sum.1), calls=%async_computation | async-start | bytes 524288 | tf_op jit(solution)/shard_map/all_to_all | solution.py:327
  14.8 0.0 copy-done
  14.8 1.9 %side.1 = (f32[1,256]{1,0:T(1,128)S(1)}, bf16[2,1024,256]{2,1,0:T(8,128)(2,1)S(1)}, bf16[2,1024,256]{2,1,0:T(8,128)(2,1)S(1)}, bf16[2,1024,256]{2,1,0:T(8,128)(2,1)S(1)}) custom-call(s32[32,128]{1,0:T(8,128)S(1)} %bitcast.9, bf16[4,2,2,1024,256]{4,3,2,1,0:T(8,128)(2,1)} %refs_2_.2), custom_call_target="tpu_custom_call" | custom-call | flops 10000000 | bytes 8388608 | tf_op jit(solution)/shard_map/side/pallas_call | solution.py:332
  16.7 7.8 %all-to-all-done.refs_0_ = bf16[32,16,256]{2,1,0:T(8,128)(2,1)S(1)} async-done(((bf16[32,16,256]{2,1,0:T(8,128)(2,1)}), bf16[32,16,256]{2,1,0:T(8,128)(2,1)S(1)}, u32[]{:S(2)}, u32[]{:S(2)}) %all-to-all-start) | async-done | bytes 262176 | tf_op jit(solution)/shard_map/all_to_all | solution.py:327
  24.4 0.0 copy-start.1
  24.4 3.0 %beam.1 = (f32[16,1024]{1,0:T(8,128)S(1)}, bf16[16,1024]{1,0:T(8,128)(2,1)S(1)}) custom-call(bf16[32,16,256]{2,1,0:T(8,128)(2,1)S(1)} %all-to-all-done.refs_0_, f32[1,256]{1,0:T(1,128)S(1)} %get-tuple-element.20.refs_1_, bf16[4,2,2,1024,256]{4,3,2,1,0:T(8,128)(2,1)} %refs_2_.2, bf16[2,1024,256]{2,1,0:T(8,128)(2,1)S(1)} %get-tuple-element.21.refs_3_, ...), custom_call_target="tpu_custom_call" | custom-call | tf_op jit(solution)/shard_map/beam/pallas_call | solution.py:347
  27.5 0.0 copy-start.2
  27.5 2.8 %collective-permute-start.3 = (bf16[16,1024]{1,0:T(8,128)(2,1)S(1)}, bf16[16,1024]{1,0:T(8,128)(2,1)S(1)}, u32[]{:S(2)}, u32[]{:S(2)}) collective-permute-start(bf16[16,1024]{1,0:T(8,128)(2,1)S(1)} %get-tuple-element.25), channel_id=1, source_target_pairs={{0,3},{1,0},{2,1},{3,2},{4,7},{5,4},{6,5},{7,6},{8,11},{9,8},{10,9... | collective-permute-start | bytes 98312 | tf_op jit(solution)/shard_map/ppermute | solution.py:364
  30.3 0.4 collective-permute-start.2
  30.6 0.7 %collective-permute-start.1 = (bf16[16,1024]{1,0:T(8,128)(2,1)S(1)}, bf16[16,1024]{1,0:T(8,128)(2,1)S(1)}, u32[]{:S(2)}, u32[]{:S(2)}) collective-permute-start(bf16[16,1024]{1,0:T(8,128)(2,1)S(1)} %get-tuple-element.25), channel_id=1, source_target_pairs={{0,1},{1,2},{2,3},{3,0},{4,5},{5,6},{6,7},{7,4},{8,9},{9,10},{10,1... | collective-permute-start | bytes 98312 | tf_op jit(solution)/shard_map/ppermute | solution.py:364
  31.3 0.0 copy-done.1
  31.3 2.1 %middle.1 = (bf16[4,1024,256]{2,1,0:T(8,128)(2,1)S(1)}, f32[4,2,16,256]{3,2,1,0:T(8,128)S(1)}, bf16[4,512,256]{2,1,0:T(8,128)(2,1)S(1)}) custom-call(s32[4]{0:T(128)S(1)} %copy-done.1, f32[16,1024]{1,0:T(8,128)S(1)} %get-tuple-element.24.refs_1_, bf16[4,1024,256]{2,1,0:T(8,128)(2,1)} %refs_2_.3), custom_call_target="tpu_custom_call" | custom-call | flops 10000000 | bytes 4200000 | tf_op jit(solution)/shard_map/middle/pallas_call | solution.py:367
  33.5 0.0 collective-permute-done.3.refs_4_
  33.5 1.1 %collective-permute-done.2.refs_3_ = bf16[16,1024]{1,0:T(8,128)(2,1)S(1)} collective-permute-done((bf16[16,1024]{1,0:T(8,128)(2,1)S(1)}, bf16[16,1024]{1,0:T(8,128)(2,1)S(1)}, u32[]{:S(2)}, u32[]{:S(2)}) %collective-permute-start.2) | collective-permute-done | bytes 32800 | tf_op jit(solution)/shard_map/ppermute | solution.py:364
  34.6 0.3 collective-permute-done.1.refs_2_
  34.9 0.0 copy-done.2
  34.9 1.2 %legendre.1 = f32[64,1,64]{2,1,0:T(1,128)S(1)} custom-call(s32[4]{0:T(128)S(1)} %copy-done.2, f32[16,1024]{1,0:T(8,128)S(1)} %get-tuple-element.24.refs_1_, bf16[16,1024]{1,0:T(8,128)(2,1)S(1)} %collective-permute-done.1.refs_2_, bf16[16,1024]{1,0:T(8,128)(2,1)S(1)} %collective-permute-done.2.refs_3_, bf16[16,1024]{1,0:T(8,128)(2,1)S(1)} %collective-permute-done.3.refs_4_, ...), custom_call_target="tpu_custom_call" | custom-call | tf_op jit(solution)/shard_map/legendre/pallas_call | solution.py:383
  36.1 18.8 %all_to_all.10.refs_1_ = f32[64,1,64]{2,1,0:T(1,128)S(1)} all-to-all(f32[64,1,64]{2,1,0:T(1,128)S(1)} %legendre.1), channel_id=1, replica_groups=mesh['ma'=64,'freq'=4] {'ma'}, dimensions={0} | all-to-all | bytes 32768 | tf_op jit(solution)/shard_map/all_to_all | solution.py:398
  54.9 1.6 %synthesis.1 = f32[2,4,2048]{2,1,0:T(4,128)} custom-call(s32[4]{0:T(128)S(1)} %copy-done.1, f32[64,1,64]{2,1,0:T(1,128)S(1)} %all_to_all.10.refs_1_, f32[4,2,16,256]{3,2,1,0:T(8,128)S(1)} %get-tuple-element.27.refs_2_, bf16[4,512,256]{2,1,0:T(8,128)(2,1)S(1)} %get-tuple-element.28.refs_3_), custom_call_target="tpu_custom_call" | custom-call | tf_op jit(solution)/shard_map/synthesis/pallas_call | solution.py:399
  (1 shorter events, 0.0 us)
Async XLA Ops:
  0.0 14.8 %copy-start = (s32[4096,1]{0,1:T(1,128)S(1)}, s32[4096,1]{0,1:T(1,128)}, u32[]{:S(2)}) copy-start(s32[4096,1]{0,1:T(1,128)} %param.8) | copy-start | bytes 49156
  0.0 4.4 %collective-permute-start = (bf16[32,2,2,256]{3,2,1,0:T(2,128)(2,1)}, bf16[32,2,2,256]{3,2,1,0:T(2,128)(2,1)S(1)}, u32[]{:S(2)}, u32[]{:S(2)}) collective-permute-start(bf16[32,2,2,256]{3,2,1,0:T(2,128)(2,1)} %signal_ref.1), channel_id=1, source_target_pairs={{0,4},{4,0},{8,12},{12,8},{16,20},{20,16},{24,28},{28,24},{32,36},... | collective-permute-start | bytes 196616 | tf_op jit(solution)/shard_map/ppermute | solution.py:295
  5.4 19.0 %all-to-all-start = ((bf16[32,16,256]{2,1,0:T(8,128)(2,1)}), bf16[32,16,256]{2,1,0:T(8,128)(2,1)S(1)}, u32[]{:S(2)}, u32[]{:S(2)}) async-start(bf16[32,16,256]{2,1,0:T(8,128)(2,1)} %time_sum.1), calls=%async_computation | async-start | bytes 524288 | tf_op jit(solution)/shard_map/all_to_all | solution.py:327
  24.4 6.9 %copy-start.1 = (s32[4]{0:T(128)S(1)}, s32[4]{0:T(128)}, u32[]{:S(2)}) copy-start(s32[4]{0:T(128)} %refs_0_.5) | copy-start | bytes 52
  27.5 7.4 %copy-start.2 = (s32[4]{0:T(128)S(1)}, s32[4]{0:T(128)}, u32[]{:S(2)}) copy-start(s32[4]{0:T(128)} %refs_0_.4) | copy-start | bytes 52
  27.5 6.0 %collective-permute-start.3 = (bf16[16,1024]{1,0:T(8,128)(2,1)S(1)}, bf16[16,1024]{1,0:T(8,128)(2,1)S(1)}, u32[]{:S(2)}, u32[]{:S(2)}) collective-permute-start(bf16[16,1024]{1,0:T(8,128)(2,1)S(1)} %get-tuple-element.25), channel_id=1, source_target_pairs={{0,3},{1,0},{2,1},{3,2},{4,7},{5,4},{6,5},{7,6},{8,11},{9,8},{10,9... | collective-permute-start | bytes 98312 | tf_op jit(solution)/shard_map/ppermute | solution.py:364
  30.3 4.3 %collective-permute-start.2 = (bf16[16,1024]{1,0:T(8,128)(2,1)S(1)}, bf16[16,1024]{1,0:T(8,128)(2,1)S(1)}, u32[]{:S(2)}, u32[]{:S(2)}) collective-permute-start(bf16[16,1024]{1,0:T(8,128)(2,1)S(1)} %get-tuple-element.25), channel_id=1, source_target_pairs={{0,2},{1,3},{2,0},{3,1},{4,6},{5,7},{6,4},{7,5},{8,10},{9,11},{10,... | collective-permute-start | bytes 98312 | tf_op jit(solution)/shard_map/ppermute | solution.py:364
  30.6 4.3 %collective-permute-start.1 = (bf16[16,1024]{1,0:T(8,128)(2,1)S(1)}, bf16[16,1024]{1,0:T(8,128)(2,1)S(1)}, u32[]{:S(2)}, u32[]{:S(2)}) collective-permute-start(bf16[16,1024]{1,0:T(8,128)(2,1)S(1)} %get-tuple-element.25), channel_id=1, source_target_pairs={{0,1},{1,2},{2,3},{3,0},{4,5},{5,6},{6,7},{7,4},{8,9},{9,10},{10,1... | collective-permute-start | bytes 98312 | tf_op jit(solution)/shard_map/ppermute | solution.py:364

commit v4 on v3

--- a/solution.py
+++ b/solution.py
@@ -56,21 +56,6 @@
     return lax.dot_general(a, b, ((contract[:1], contract[1:]), ((), ())), preferred_element_type=F32)
 
 
-def call(kernel, outs, specs, *args, name=None):
-    args = [
-        pltpu.with_memory_space_constraint(a, pltpu.VMEM) if s is VMEM else a
-        for a, s in zip(args, specs)
-    ]
-    return pl.pallas_call(
-        kernel,
-        out_shape=tuple(pltpu.VMEM(s, d) for s, d in outs),
-        in_specs=list(specs),
-        out_specs=tuple(VMEM for _ in outs),
-        compiler_params=PARAMS,
-        name=name,
-    )(*args)
-
-
 def phase_table(modes, mode_dev, nfreq, chip_times, ntime):
     half = modes // 2
     row = np.arange(2 * half * nfreq)[:, None]
@@ -109,7 +94,7 @@
 
 
 def time_kernel(nfreq, chips, mode_dev, table_ref, *refs):
-    *signal_refs, out_ref = refs
+    *signal_refs, out_ref, part_ref, semaphores = refs
     place = lax.axis_index("ma")
     core = lax.rem(place, 2)
     own_left, own_right, other_left, other_right = (ref[...] for ref in signal_refs)
@@ -127,9 +112,19 @@
     square = turn * turn
     cosine, sine = polynomial(square, COS)[None], (polynomial(square, SIN) * turn)[None]
     real, imag = total.reshape(2, -1, period, width)
-    shape = (dests, rows // 2, width)
-    real, imag = real * cosine + imag * sine, imag * cosine - real * sine
-    out_ref[...] = jnp.concatenate([real.reshape(shape), imag.reshape(shape)], 1).astype(BF16)
+    parts = semaphores.shape[0]
+    blocks, size = real.shape[0] // parts, dests // parts
+    shape = (size, rows // 2, width)
+    copies = []
+    for i in range(parts):
+        a, b = real[i * blocks : (i + 1) * blocks], imag[i * blocks : (i + 1) * blocks]
+        a, b = a * cosine + b * sine, b * cosine - a * sine
+        at = pl.ds(i * size, size)
+        part_ref[at] = jnp.concatenate([a.reshape(shape), b.reshape(shape)], 1).astype(BF16)
+        copies.append(pltpu.make_async_copy(part_ref.at[at], out_ref.at[at], semaphores.at[i]))
+        copies[i].start()
+    for copy in copies:
+        copy.wait()
 
 
 def side_kernel(nfreq, pair_ref, beam_ref, weight_ref, *refs):
@@ -247,7 +242,9 @@
     copy.wait()
 
 
-def synthesis_kernel(nfreq, count_ref, value_ref, outer_ref, inner_ref, map_ref):
+def synthesis_kernel(
+    nfreq, count_ref, value_ref, outer_ref, inner_ref, out_ref, map_ref, semaphores
+):
     circles = outer_ref.shape[0]
     sources, _, width = value_ref.shape
     values = value_ref[...].reshape(sources, width).T
@@ -273,12 +270,17 @@
             result[:half, :INNER] + (result[:half, INNER:] + result[half:, :INNER])
         )
     pixel = iota((OUTER, INNER), 0) * INNER + iota((OUTER, INNER), 1)
-    for circle in range(circles):
-        keep = pixel < count_ref[circle]
-        for f in range(nfreq):
+    copies = []
+    for f in range(nfreq):
+        for circle in range(circles):
+            keep = pixel < count_ref[circle]
             part = jnp.where(keep, results[circle][f * OUTER : (f + 1) * OUTER], 0.0)
             for q in range(OUTER):
                 map_ref[f, circle : circle + 1, q * INNER : (q + 1) * INNER] = part[q : q + 1]
+        copies.append(pltpu.make_async_copy(map_ref.at[f], out_ref.at[f], semaphores.at[f]))
+        copies[f].start()
+    for copy in copies:
+        copy.wait()
 
 
 def body(visibility, pair_baseline, beam_inverse, block_rows, legendre, circle_pixels):
@@ -312,16 +314,26 @@
         pltpu.with_memory_space_constraint(table, pltpu.HBM),
         pltpu.with_memory_space_constraint(visibility, pltpu.HBM),
     )
-    (partial_spectrum,) = call(
+    spectrum_shape = (ma_count // 2, rows, base_dev)
+    partial_spectrum = pl.pallas_call(
         lambda *refs: time_kernel(nfreq, ma_count // 2, mode_dev, *refs),
-        [((ma_count // 2, rows, base_dev), BF16)],
-        [VMEM] * 5,
-        near,
+        out_shape=jax.ShapeDtypeStruct(spectrum_shape, BF16),
+        in_specs=[VMEM] * 5,
+        out_specs=ANY,
+        scratch_shapes=[pltpu.VMEM(spectrum_shape, BF16), pltpu.SemaphoreType.DMA((4,))],
+        compiler_params=PARAMS,
+        name="time_sum",
+    )(
         *(
-            a.reshape(-1, base_half)
-            for a in (left, right, other[..., :base_half], other[..., base_half:])
-        ),
-        name="time_sum",
+            pltpu.with_memory_space_constraint(a, pltpu.VMEM)
+            for a in (
+                near,
+                *(
+                    a.reshape(-1, base_half)
+                    for a in (left, right, other[..., :base_half], other[..., base_half:])
+                ),
+            )
+        )
     )
     groups = [list(range(core, ma_count, 2)) for core in range(2)]
     received = lax.all_to_all(partial_spectrum, "ma", 0, 0, axis_index_groups=groups)
@@ -400,7 +412,11 @@
         lambda *refs: synthesis_kernel(nfreq, *refs),
         out_shape=jax.ShapeDtypeStruct((nfreq, circles, PMAX), F32),
         in_specs=[SMEM, VMEM, VMEM, VMEM],
-        out_specs=VMEM,
+        out_specs=ANY,
+        scratch_shapes=[
+            pltpu.VMEM((nfreq, circles, PMAX), F32),
+            pltpu.SemaphoreType.DMA((nfreq,)),
+        ],
         compiler_params=PARAMS,
         name="synthesis",
     )(

time: 56.8 us -> 56.8 us (level)
  no operation moved by 1% of the time
where the time goes in v4:
time: 56.8 us; the launch traced here: 56.5 us
  blocking collectives  18.8 us (33%)
  starting transfers between devices  16.4 us (29%)
  Pallas kernels  11.9 us (21%)
  waiting for transfers between devices  9.19 us (16%)
    all_to_all x1, blocking collectives, body(): regrouped = lax.all_to_all(latitude, 'ma', 0, 0)  18.8 us
    all_to_all x1, starting transfers between devices, body(): lax.all_to_all(partial_spectrum, 'ma', 0, 0, axis_index_groups=groups)  9.32 us
    all_to_all x1, waiting for transfers between devices, body(): lax.all_to_all(partial_spectrum, 'ma', 0, 0, axis_index_groups=groups)  7.77 us
    ppermute x3, starting transfers between devices, body(): lax.ppermute(send, 'freq', [(i, (i + k) % freq_count) for i in range(freq...  3.85 us
    ppermute x1, starting transfers between devices, body(): lax.ppermute(visibility, 'ma', [(i, i ^ 1) for i in range(ma_count)])  3.24 us
    pallas_call x1, Pallas kernels, body(): pl.pallas_call(lambda *refs: beam_kernel(nfreq, *refs), out_shape=(pltpu....  3.02 us
    pallas_call x1, Pallas kernels, body(): pl.pallas_call(lambda *refs: middle_kernel(modes, mode_dev, *refs), out_s...  2.14 us
    pallas_call x1, Pallas kernels, body(): pl.pallas_call(lambda *refs: side_kernel(nfreq, *refs), out_shape=(pltpu....  1.89 us
  transfers between devices with their start and end apart: 5, of which 3 were waited for; matrix products, arithmetic and copies ran while one was open for 0% of the time, Pallas kernels for 9%

profile of v4, /device:TPU:1, one launch (start us, length us, event | category | flops | bytes accessed | tf_op | source)
XLA Modules:
  0.0 56.5 jit_solution(10626047702721307301)
XLA Ops:
  0.0 0.0 copy-start
  0.0 3.2 %collective-permute-start = (bf16[32,2,2,256]{3,2,1,0:T(2,128)(2,1)}, bf16[32,2,2,256]{3,2,1,0:T(2,128)(2,1)S(1)}, u32[]{:S(2)}, u32[]{:S(2)}) collective-permute-start(bf16[32,2,2,256]{3,2,1,0:T(2,128)(2,1)} %signal_ref.1), channel_id=1, source_target_pairs={{0,4},{4,0},{8,12},{12,8},{16,20},{20,16},{24,28},{28,24},{32,36},... | collective-permute-start | bytes 196616 | tf_op jit(solution)/shard_map/ppermute | solution.py:297
  3.2 1.1 %fetch.1 = (bf16[2,512,256]{2,1,0:T(8,128)(2,1)S(1)}, bf16[32,2,2,128]{3,2,1,0:T(2,128)(2,1)S(1)}, bf16[32,2,2,128]{3,2,1,0:T(2,128)(2,1)S(1)}) custom-call(bf16[2,2,512,256]{3,2,1,0:T(8,128)(2,1)} %constant.2.clone.table_ref, bf16[32,2,2,256]{3,2,1,0:T(2,128)(2,1)} %signal_ref.1), custom_call_target="tpu_custom_call" | custom-call | bytes 1200000 | tf_op jit(solution)/shard_map/fetch/pallas_call | solution.py:300
  4.4 0.0 collective-permute-done
  4.4 1.0 %time_sum.1 = bf16[32,16,256]{2,1,0:T(8,128)(2,1)} custom-call(bf16[2,512,256]{2,1,0:T(8,128)(2,1)S(1)} %get-tuple-element.17.refs_0_, bf16[128,128]{1,0:T(8,128)(2,1)S(1)} %bitcast.7, bf16[128,128]{1,0:T(8,128)(2,1)S(1)} %bitcast.8, bf16[128,128]{1,0:T(8,128)(2,1)S(1)} %bitcast.6, bf16[128,128]{1,0:T(8,128)(2,1)S(1)} %bitcast.5), custom_call_target="tpu_custom_call" | custom-call | tf_op jit(solution)/shard_map/time_sum/pallas_call | solution.py:318
  5.4 9.3 %all-to-all-start = ((bf16[32,16,256]{2,1,0:T(8,128)(2,1)}), bf16[32,16,256]{2,1,0:T(8,128)(2,1)S(1)}, u32[]{:S(2)}, u32[]{:S(2)}) async-start(bf16[32,16,256]{2,1,0:T(8,128)(2,1)} %time_sum.1), calls=%async_computation | async-start | bytes 524288 | tf_op jit(solution)/shard_map/all_to_all | solution.py:339
  14.8 0.0 copy-done
  14.8 1.9 %side.1 = (f32[1,256]{1,0:T(1,128)S(1)}, bf16[2,1024,256]{2,1,0:T(8,128)(2,1)S(1)}, bf16[2,1024,256]{2,1,0:T(8,128)(2,1)S(1)}, bf16[2,1024,256]{2,1,0:T(8,128)(2,1)S(1)}) custom-call(s32[32,128]{1,0:T(8,128)S(1)} %bitcast.9, bf16[4,2,2,1024,256]{4,3,2,1,0:T(8,128)(2,1)} %refs_2_.2), custom_call_target="tpu_custom_call" | custom-call | flops 10000000 | bytes 8388608 | tf_op jit(solution)/shard_map/side/pallas_call | solution.py:344
  16.7 7.8 %all-to-all-done.refs_0_ = bf16[32,16,256]{2,1,0:T(8,128)(2,1)S(1)} async-done(((bf16[32,16,256]{2,1,0:T(8,128)(2,1)}), bf16[32,16,256]{2,1,0:T(8,128)(2,1)S(1)}, u32[]{:S(2)}, u32[]{:S(2)}) %all-to-all-start) | async-done | bytes 262176 | tf_op jit(solution)/shard_map/all_to_all | solution.py:339
  24.4 0.0 copy-start.1
  24.4 3.0 %beam.1 = (f32[16,1024]{1,0:T(8,128)S(1)}, bf16[16,1024]{1,0:T(8,128)(2,1)S(1)}) custom-call(bf16[32,16,256]{2,1,0:T(8,128)(2,1)S(1)} %all-to-all-done.refs_0_, f32[1,256]{1,0:T(1,128)S(1)} %get-tuple-element.20.refs_1_, bf16[4,2,2,1024,256]{4,3,2,1,0:T(8,128)(2,1)} %refs_2_.2, bf16[2,1024,256]{2,1,0:T(8,128)(2,1)S(1)} %get-tuple-element.21.refs_3_, ...), custom_call_target="tpu_custom_call" | custom-call | tf_op jit(solution)/shard_map/beam/pallas_call | solution.py:359
  27.5 0.0 copy-start.2
  27.5 2.8 %collective-permute-start.3 = (bf16[16,1024]{1,0:T(8,128)(2,1)S(1)}, bf16[16,1024]{1,0:T(8,128)(2,1)S(1)}, u32[]{:S(2)}, u32[]{:S(2)}) collective-permute-start(bf16[16,1024]{1,0:T(8,128)(2,1)S(1)} %get-tuple-element.25), channel_id=1, source_target_pairs={{0,3},{1,0},{2,1},{3,2},{4,7},{5,4},{6,5},{7,6},{8,11},{9,8},{10,9... | collective-permute-start | bytes 98312 | tf_op jit(solution)/shard_map/ppermute | solution.py:376
  30.3 0.3 collective-permute-start.2
  30.6 0.7 %collective-permute-start.1 = (bf16[16,1024]{1,0:T(8,128)(2,1)S(1)}, bf16[16,1024]{1,0:T(8,128)(2,1)S(1)}, u32[]{:S(2)}, u32[]{:S(2)}) collective-permute-start(bf16[16,1024]{1,0:T(8,128)(2,1)S(1)} %get-tuple-element.25), channel_id=1, source_target_pairs={{0,1},{1,2},{2,3},{3,0},{4,5},{5,6},{6,7},{7,4},{8,9},{9,10},{10,1... | collective-permute-start | bytes 98312 | tf_op jit(solution)/shard_map/ppermute | solution.py:376
  31.3 0.0 copy-done.1
  31.3 2.1 %middle.1 = (bf16[4,1024,256]{2,1,0:T(8,128)(2,1)S(1)}, f32[4,2,16,256]{3,2,1,0:T(8,128)S(1)}, bf16[4,512,256]{2,1,0:T(8,128)(2,1)S(1)}) custom-call(s32[4]{0:T(128)S(1)} %copy-done.1, f32[16,1024]{1,0:T(8,128)S(1)} %get-tuple-element.24.refs_1_, bf16[4,1024,256]{2,1,0:T(8,128)(2,1)} %refs_2_.3), custom_call_target="tpu_custom_call" | custom-call | flops 10000000 | bytes 4200000 | tf_op jit(solution)/shard_map/middle/pallas_call | solution.py:379
  33.5 0.0 collective-permute-done.3.refs_4_
  33.5 1.1 %collective-permute-done.2.refs_3_ = bf16[16,1024]{1,0:T(8,128)(2,1)S(1)} collective-permute-done((bf16[16,1024]{1,0:T(8,128)(2,1)S(1)}, bf16[16,1024]{1,0:T(8,128)(2,1)S(1)}, u32[]{:S(2)}, u32[]{:S(2)}) %collective-permute-start.2) | collective-permute-done | bytes 32800 | tf_op jit(solution)/shard_map/ppermute | solution.py:376
  34.6 0.3 collective-permute-done.1.refs_2_
  34.9 0.0 copy-done.2
  34.9 1.2 %legendre.1 = f32[64,1,64]{2,1,0:T(1,128)S(1)} custom-call(s32[4]{0:T(128)S(1)} %copy-done.2, f32[16,1024]{1,0:T(8,128)S(1)} %get-tuple-element.24.refs_1_, bf16[16,1024]{1,0:T(8,128)(2,1)S(1)} %collective-permute-done.1.refs_2_, bf16[16,1024]{1,0:T(8,128)(2,1)S(1)} %collective-permute-done.2.refs_3_, bf16[16,1024]{1,0:T(8,128)(2,1)S(1)} %collective-permute-done.3.refs_4_, ...), custom_call_target="tpu_custom_call" | custom-call | tf_op jit(solution)/shard_map/legendre/pallas_call | solution.py:395
  36.1 18.8 %all_to_all.10.refs_1_ = f32[64,1,64]{2,1,0:T(1,128)S(1)} all-to-all(f32[64,1,64]{2,1,0:T(1,128)S(1)} %legendre.1), channel_id=1, replica_groups=mesh['ma'=64,'freq'=4] {'ma'}, dimensions={0} | all-to-all | bytes 32768 | tf_op jit(solution)/shard_map/all_to_all | solution.py:410
  54.9 1.6 %synthesis.1 = f32[2,4,2048]{2,1,0:T(4,128)} custom-call(s32[4]{0:T(128)S(1)} %copy-done.1, f32[64,1,64]{2,1,0:T(1,128)S(1)} %all_to_all.10.refs_1_, f32[4,2,16,256]{3,2,1,0:T(8,128)S(1)} %get-tuple-element.27.refs_2_, bf16[4,512,256]{2,1,0:T(8,128)(2,1)S(1)} %get-tuple-element.28.refs_3_), custom_call_target="tpu_custom_call" | custom-call | tf_op jit(solution)/shard_map/synthesis/pallas_call | solution.py:411
  (1 shorter events, 0.0 us)
Async XLA Ops:
  0.0 14.8 %copy-start = (s32[4096,1]{0,1:T(1,128)S(1)}, s32[4096,1]{0,1:T(1,128)}, u32[]{:S(2)}) copy-start(s32[4096,1]{0,1:T(1,128)} %param.8) | copy-start | bytes 49156
  0.0 4.4 %collective-permute-start = (bf16[32,2,2,256]{3,2,1,0:T(2,128)(2,1)}, bf16[32,2,2,256]{3,2,1,0:T(2,128)(2,1)S(1)}, u32[]{:S(2)}, u32[]{:S(2)}) collective-permute-start(bf16[32,2,2,256]{3,2,1,0:T(2,128)(2,1)} %signal_ref.1), channel_id=1, source_target_pairs={{0,4},{4,0},{8,12},{12,8},{16,20},{20,16},{24,28},{28,24},{32,36},... | collective-permute-start | bytes 196616 | tf_op jit(solution)/shard_map/ppermute | solution.py:297
  5.4 19.0 %all-to-all-start = ((bf16[32,16,256]{2,1,0:T(8,128)(2,1)}), bf16[32,16,256]{2,1,0:T(8,128)(2,1)S(1)}, u32[]{:S(2)}, u32[]{:S(2)}) async-start(bf16[32,16,256]{2,1,0:T(8,128)(2,1)} %time_sum.1), calls=%async_computation | async-start | bytes 524288 | tf_op jit(solution)/shard_map/all_to_all | solution.py:339
  24.4 6.9 %copy-start.1 = (s32[4]{0:T(128)S(1)}, s32[4]{0:T(128)}, u32[]{:S(2)}) copy-start(s32[4]{0:T(128)} %refs_0_.5) | copy-start | bytes 52
  27.5 7.4 %copy-start.2 = (s32[4]{0:T(128)S(1)}, s32[4]{0:T(128)}, u32[]{:S(2)}) copy-start(s32[4]{0:T(128)} %refs_0_.4) | copy-start | bytes 52
  27.5 6.0 %collective-permute-start.3 = (bf16[16,1024]{1,0:T(8,128)(2,1)S(1)}, bf16[16,1024]{1,0:T(8,128)(2,1)S(1)}, u32[]{:S(2)}, u32[]{:S(2)}) collective-permute-start(bf16[16,1024]{1,0:T(8,128)(2,1)S(1)} %get-tuple-element.25), channel_id=1, source_target_pairs={{0,3},{1,0},{2,1},{3,2},{4,7},{5,4},{6,5},{7,6},{8,11},{9,8},{10,9... | collective-permute-start | bytes 98312 | tf_op jit(solution)/shard_map/ppermute | solution.py:376
  30.3 4.3 %collective-permute-start.2 = (bf16[16,1024]{1,0:T(8,128)(2,1)S(1)}, bf16[16,1024]{1,0:T(8,128)(2,1)S(1)}, u32[]{:S(2)}, u32[]{:S(2)}) collective-permute-start(bf16[16,1024]{1,0:T(8,128)(2,1)S(1)} %get-tuple-element.25), channel_id=1, source_target_pairs={{0,2},{1,3},{2,0},{3,1},{4,6},{5,7},{6,4},{7,5},{8,10},{9,11},{10,... | collective-permute-start | bytes 98312 | tf_op jit(solution)/shard_map/ppermute | solution.py:376
  30.6 4.3 %collective-permute-start.1 = (bf16[16,1024]{1,0:T(8,128)(2,1)S(1)}, bf16[16,1024]{1,0:T(8,128)(2,1)S(1)}, u32[]{:S(2)}, u32[]{:S(2)}) collective-permute-start(bf16[16,1024]{1,0:T(8,128)(2,1)S(1)} %get-tuple-element.25), channel_id=1, source_target_pairs={{0,1},{1,2},{2,3},{3,0},{4,5},{5,6},{6,7},{7,4},{8,9},{9,10},{10,1... | collective-permute-start | bytes 98312 | tf_op jit(solution)/shard_map/ppermute | solution.py:376

commit v5 on v3

--- a/solution.py
+++ b/solution.py
@@ -238,13 +238,18 @@
 
 def middle_kernel(
     modes, mode_dev, count_ref, after_ref, legendre_ref,
-    near_ref, outer_ref, inner_ref, semaphore,
+    near_ref, outer_ref, inner_ref, semaphores,
 ):
     del after_ref
-    copy = pltpu.make_async_copy(legendre_ref, near_ref, semaphore)
-    copy.start()
+    copies = [
+        pltpu.make_async_copy(legendre_ref.at[m], near_ref.at[m], semaphores.at[m])
+        for m in range(near_ref.shape[0])
+    ]
+    for copy in copies:
+        copy.start()
     table_kernel(modes, mode_dev, count_ref, outer_ref, inner_ref)
-    copy.wait()
+    for copy in copies:
+        copy.wait()
 
 
 def synthesis_kernel(nfreq, count_ref, value_ref, outer_ref, inner_ref, map_ref):
@@ -373,7 +378,7 @@
         ),
         in_specs=[SMEM, ANY, ANY],
         out_specs=(VMEM,) * 3,
-        scratch_shapes=[pltpu.SemaphoreType.DMA(())],
+        scratch_shapes=[pltpu.SemaphoreType.DMA((mode_dev,))],
         compiler_params=PARAMS,
         cost_estimate=pl.CostEstimate(
             flops=10000000, bytes_accessed=4200000, transcendentals=0

time: 56.8 us -> 56.8 us (level)
  no operation moved by 1% of the time
where the time goes in v5:
time: 56.8 us; the launch traced here: 56.5 us
  blocking collectives  18.8 us (33%)
  starting transfers between devices  16.4 us (29%)
  Pallas kernels  11.9 us (21%)
  waiting for transfers between devices  9.24 us (16%)
    all_to_all x1, blocking collectives, body(): regrouped = lax.all_to_all(latitude, 'ma', 0, 0)  18.8 us
    all_to_all x1, starting transfers between devices, body(): lax.all_to_all(partial_spectrum, 'ma', 0, 0, axis_index_groups=groups)  9.31 us
    all_to_all x1, waiting for transfers between devices, body(): lax.all_to_all(partial_spectrum, 'ma', 0, 0, axis_index_groups=groups)  7.77 us
    ppermute x3, starting transfers between devices, body(): lax.ppermute(send, 'freq', [(i, (i + k) % freq_count) for i in range(freq...  3.85 us
    ppermute x1, starting transfers between devices, body(): lax.ppermute(visibility, 'ma', [(i, i ^ 1) for i in range(ma_count)])  3.24 us
    pallas_call x1, Pallas kernels, body(): pl.pallas_call(lambda *refs: beam_kernel(nfreq, *refs), out_shape=(pltpu....  3.02 us
    pallas_call x1, Pallas kernels, body(): pl.pallas_call(lambda *refs: middle_kernel(modes, mode_dev, *refs), out_s...  2.09 us
    pallas_call x1, Pallas kernels, body(): pl.pallas_call(lambda *refs: side_kernel(nfreq, *refs), out_shape=(pltpu....  1.89 us
  transfers between devices with their start and end apart: 5, of which 3 were waited for; matrix products, arithmetic and copies ran while one was open for 0% of the time, Pallas kernels for 9%

profile of v5, /device:TPU:1, one launch (start us, length us, event | category | flops | bytes accessed | tf_op | source)
XLA Modules:
  0.0 56.5 jit_solution(2322864802384784349)
XLA Ops:
  0.0 0.0 copy-start
  0.0 3.2 %collective-permute-start = (bf16[32,2,2,256]{3,2,1,0:T(2,128)(2,1)}, bf16[32,2,2,256]{3,2,1,0:T(2,128)(2,1)S(1)}, u32[]{:S(2)}, u32[]{:S(2)}) collective-permute-start(bf16[32,2,2,256]{3,2,1,0:T(2,128)(2,1)} %signal_ref.1), channel_id=1, source_target_pairs={{0,4},{4,0},{8,12},{12,8},{16,20},{20,16},{24,28},{28,24},{32,36},... | collective-permute-start | bytes 196616 | tf_op jit(solution)/shard_map/ppermute | solution.py:300
  3.2 1.1 %fetch.1 = (bf16[2,512,256]{2,1,0:T(8,128)(2,1)S(1)}, bf16[32,2,2,128]{3,2,1,0:T(2,128)(2,1)S(1)}, bf16[32,2,2,128]{3,2,1,0:T(2,128)(2,1)S(1)}) custom-call(bf16[2,2,512,256]{3,2,1,0:T(8,128)(2,1)} %constant.2.clone.table_ref, bf16[32,2,2,256]{3,2,1,0:T(2,128)(2,1)} %signal_ref.1), custom_call_target="tpu_custom_call" | custom-call | bytes 1200000 | tf_op jit(solution)/shard_map/fetch/pallas_call | solution.py:303
  4.4 0.0 collective-permute-done
  4.4 1.0 %time_sum.1 = bf16[32,16,256]{2,1,0:T(8,128)(2,1)} custom-call(bf16[2,512,256]{2,1,0:T(8,128)(2,1)S(1)} %get-tuple-element.17.refs_0_, bf16[128,128]{1,0:T(8,128)(2,1)S(1)} %bitcast.7, bf16[128,128]{1,0:T(8,128)(2,1)S(1)} %bitcast.8, bf16[128,128]{1,0:T(8,128)(2,1)S(1)} %bitcast.6, bf16[128,128]{1,0:T(8,128)(2,1)S(1)} %bitcast.5), custom_call_target="tpu_custom_call" | custom-call | tf_op jit(solution)/shard_map/time_sum/pallas_call | solution.py:64
  5.4 9.3 %all-to-all-start = ((bf16[32,16,256]{2,1,0:T(8,128)(2,1)}), bf16[32,16,256]{2,1,0:T(8,128)(2,1)S(1)}, u32[]{:S(2)}, u32[]{:S(2)}) async-start(bf16[32,16,256]{2,1,0:T(8,128)(2,1)} %time_sum.1), calls=%async_computation | async-start | bytes 524288 | tf_op jit(solution)/shard_map/all_to_all | solution.py:332
  14.8 0.0 copy-done
  14.8 1.9 %side.1 = (f32[1,256]{1,0:T(1,128)S(1)}, bf16[2,1024,256]{2,1,0:T(8,128)(2,1)S(1)}, bf16[2,1024,256]{2,1,0:T(8,128)(2,1)S(1)}, bf16[2,1024,256]{2,1,0:T(8,128)(2,1)S(1)}) custom-call(s32[32,128]{1,0:T(8,128)S(1)} %bitcast.9, bf16[4,2,2,1024,256]{4,3,2,1,0:T(8,128)(2,1)} %refs_2_.2), custom_call_target="tpu_custom_call" | custom-call | flops 10000000 | bytes 8388608 | tf_op jit(solution)/shard_map/side/pallas_call | solution.py:337
  16.7 7.8 %all-to-all-done.refs_0_ = bf16[32,16,256]{2,1,0:T(8,128)(2,1)S(1)} async-done(((bf16[32,16,256]{2,1,0:T(8,128)(2,1)}), bf16[32,16,256]{2,1,0:T(8,128)(2,1)S(1)}, u32[]{:S(2)}, u32[]{:S(2)}) %all-to-all-start) | async-done | bytes 262176 | tf_op jit(solution)/shard_map/all_to_all | solution.py:332
  24.4 0.0 copy-start.1
  24.4 3.0 %beam.1 = (f32[16,1024]{1,0:T(8,128)S(1)}, bf16[16,1024]{1,0:T(8,128)(2,1)S(1)}) custom-call(bf16[32,16,256]{2,1,0:T(8,128)(2,1)S(1)} %all-to-all-done.refs_0_, f32[1,256]{1,0:T(1,128)S(1)} %get-tuple-element.20.refs_1_, bf16[4,2,2,1024,256]{4,3,2,1,0:T(8,128)(2,1)} %refs_2_.2, bf16[2,1024,256]{2,1,0:T(8,128)(2,1)S(1)} %get-tuple-element.21.refs_3_, ...), custom_call_target="tpu_custom_call" | custom-call | tf_op jit(solution)/shard_map/beam/pallas_call | solution.py:352
  27.5 0.0 copy-start.2
  27.5 2.8 %collective-permute-start.3 = (bf16[16,1024]{1,0:T(8,128)(2,1)S(1)}, bf16[16,1024]{1,0:T(8,128)(2,1)S(1)}, u32[]{:S(2)}, u32[]{:S(2)}) collective-permute-start(bf16[16,1024]{1,0:T(8,128)(2,1)S(1)} %get-tuple-element.25), channel_id=1, source_target_pairs={{0,3},{1,0},{2,1},{3,2},{4,7},{5,4},{6,5},{7,6},{8,11},{9,8},{10,9... | collective-permute-start | bytes 98312 | tf_op jit(solution)/shard_map/ppermute | solution.py:369
  30.3 0.4 collective-permute-start.2
  30.6 0.7 %collective-permute-start.1 = (bf16[16,1024]{1,0:T(8,128)(2,1)S(1)}, bf16[16,1024]{1,0:T(8,128)(2,1)S(1)}, u32[]{:S(2)}, u32[]{:S(2)}) collective-permute-start(bf16[16,1024]{1,0:T(8,128)(2,1)S(1)} %get-tuple-element.25), channel_id=1, source_target_pairs={{0,1},{1,2},{2,3},{3,0},{4,5},{5,6},{6,7},{7,4},{8,9},{9,10},{10,1... | collective-permute-start | bytes 98312 | tf_op jit(solution)/shard_map/ppermute | solution.py:369
  31.3 0.0 copy-done.1
  31.3 2.1 %middle.1 = (bf16[4,1024,256]{2,1,0:T(8,128)(2,1)S(1)}, f32[4,2,16,256]{3,2,1,0:T(8,128)S(1)}, bf16[4,512,256]{2,1,0:T(8,128)(2,1)S(1)}) custom-call(s32[4]{0:T(128)S(1)} %copy-done.1, f32[16,1024]{1,0:T(8,128)S(1)} %get-tuple-element.24.refs_1_, bf16[4,1024,256]{2,1,0:T(8,128)(2,1)} %refs_2_.3), custom_call_target="tpu_custom_call" | custom-call | flops 10000000 | bytes 4200000 | tf_op jit(solution)/shard_map/middle/pallas_call | solution.py:372
  33.4 0.0 collective-permute-done.3.refs_4_
  33.4 1.1 %collective-permute-done.2.refs_3_ = bf16[16,1024]{1,0:T(8,128)(2,1)S(1)} collective-permute-done((bf16[16,1024]{1,0:T(8,128)(2,1)S(1)}, bf16[16,1024]{1,0:T(8,128)(2,1)S(1)}, u32[]{:S(2)}, u32[]{:S(2)}) %collective-permute-start.2) | collective-permute-done | bytes 32800 | tf_op jit(solution)/shard_map/ppermute | solution.py:369
  34.6 0.3 collective-permute-done.1.refs_2_
  34.9 0.0 copy-done.2
  34.9 1.2 %legendre.1 = f32[64,1,64]{2,1,0:T(1,128)S(1)} custom-call(s32[4]{0:T(128)S(1)} %copy-done.2, f32[16,1024]{1,0:T(8,128)S(1)} %get-tuple-element.24.refs_1_, bf16[16,1024]{1,0:T(8,128)(2,1)S(1)} %collective-permute-done.1.refs_2_, bf16[16,1024]{1,0:T(8,128)(2,1)S(1)} %collective-permute-done.2.refs_3_, bf16[16,1024]{1,0:T(8,128)(2,1)S(1)} %collective-permute-done.3.refs_4_, ...), custom_call_target="tpu_custom_call" | custom-call | tf_op jit(solution)/shard_map/legendre/pallas_call | solution.py:388
  36.1 18.8 %all_to_all.10.refs_1_ = f32[64,1,64]{2,1,0:T(1,128)S(1)} all-to-all(f32[64,1,64]{2,1,0:T(1,128)S(1)} %legendre.1), channel_id=1, replica_groups=mesh['ma'=64,'freq'=4] {'ma'}, dimensions={0} | all-to-all | bytes 32768 | tf_op jit(solution)/shard_map/all_to_all | solution.py:403
  54.9 1.6 %synthesis.1 = f32[2,4,2048]{2,1,0:T(4,128)} custom-call(s32[4]{0:T(128)S(1)} %copy-done.1, f32[64,1,64]{2,1,0:T(1,128)S(1)} %all_to_all.10.refs_1_, f32[4,2,16,256]{3,2,1,0:T(8,128)S(1)} %get-tuple-element.27.refs_2_, bf16[4,512,256]{2,1,0:T(8,128)(2,1)S(1)} %get-tuple-element.28.refs_3_), custom_call_target="tpu_custom_call" | custom-call | tf_op jit(solution)/shard_map/synthesis/pallas_call | solution.py:404
  (1 shorter events, 0.0 us)
Async XLA Ops:
  0.0 14.8 %copy-start = (s32[4096,1]{0,1:T(1,128)S(1)}, s32[4096,1]{0,1:T(1,128)}, u32[]{:S(2)}) copy-start(s32[4096,1]{0,1:T(1,128)} %param.8) | copy-start | bytes 49156
  0.0 4.4 %collective-permute-start = (bf16[32,2,2,256]{3,2,1,0:T(2,128)(2,1)}, bf16[32,2,2,256]{3,2,1,0:T(2,128)(2,1)S(1)}, u32[]{:S(2)}, u32[]{:S(2)}) collective-permute-start(bf16[32,2,2,256]{3,2,1,0:T(2,128)(2,1)} %signal_ref.1), channel_id=1, source_target_pairs={{0,4},{4,0},{8,12},{12,8},{16,20},{20,16},{24,28},{28,24},{32,36},... | collective-permute-start | bytes 196616 | tf_op jit(solution)/shard_map/ppermute | solution.py:300
  5.4 19.0 %all-to-all-start = ((bf16[32,16,256]{2,1,0:T(8,128)(2,1)}), bf16[32,16,256]{2,1,0:T(8,128)(2,1)S(1)}, u32[]{:S(2)}, u32[]{:S(2)}) async-start(bf16[32,16,256]{2,1,0:T(8,128)(2,1)} %time_sum.1), calls=%async_computation | async-start | bytes 524288 | tf_op jit(solution)/shard_map/all_to_all | solution.py:332
  24.4 6.9 %copy-start.1 = (s32[4]{0:T(128)S(1)}, s32[4]{0:T(128)}, u32[]{:S(2)}) copy-start(s32[4]{0:T(128)} %refs_0_.5) | copy-start | bytes 52
  27.5 7.4 %copy-start.2 = (s32[4]{0:T(128)S(1)}, s32[4]{0:T(128)}, u32[]{:S(2)}) copy-start(s32[4]{0:T(128)} %refs_0_.4) | copy-start | bytes 52
  27.5 6.0 %collective-permute-start.3 = (bf16[16,1024]{1,0:T(8,128)(2,1)S(1)}, bf16[16,1024]{1,0:T(8,128)(2,1)S(1)}, u32[]{:S(2)}, u32[]{:S(2)}) collective-permute-start(bf16[16,1024]{1,0:T(8,128)(2,1)S(1)} %get-tuple-element.25), channel_id=1, source_target_pairs={{0,3},{1,0},{2,1},{3,2},{4,7},{5,4},{6,5},{7,6},{8,11},{9,8},{10,9... | collective-permute-start | bytes 98312 | tf_op jit(solution)/shard_map/ppermute | solution.py:369
  30.3 4.3 %collective-permute-start.2 = (bf16[16,1024]{1,0:T(8,128)(2,1)S(1)}, bf16[16,1024]{1,0:T(8,128)(2,1)S(1)}, u32[]{:S(2)}, u32[]{:S(2)}) collective-permute-start(bf16[16,1024]{1,0:T(8,128)(2,1)S(1)} %get-tuple-element.25), channel_id=1, source_target_pairs={{0,2},{1,3},{2,0},{3,1},{4,6},{5,7},{6,4},{7,5},{8,10},{9,11},{10,... | collective-permute-start | bytes 98312 | tf_op jit(solution)/shard_map/ppermute | solution.py:369
  30.6 4.3 %collective-permute-start.1 = (bf16[16,1024]{1,0:T(8,128)(2,1)S(1)}, bf16[16,1024]{1,0:T(8,128)(2,1)S(1)}, u32[]{:S(2)}, u32[]{:S(2)}) collective-permute-start(bf16[16,1024]{1,0:T(8,128)(2,1)S(1)} %get-tuple-element.25), channel_id=1, source_target_pairs={{0,1},{1,2},{2,3},{3,0},{4,5},{5,6},{6,7},{7,4},{8,9},{9,10},{10,1... | collective-permute-start | bytes 98312 | tf_op jit(solution)/shard_map/ppermute | solution.py:369
